TPU v7x, 256 devices: a whole 4x4x8 slice. The times are simulated.
256 devices in a mesh: dp: 8 (over y, core), ctx: 32 (over z, x).
Axes of the slice: x: 4, y: 4, z: 8, core: 2. Of those that a mesh axis runs over, the one named last changes fastest.
Arguments:
- hidden_in: bfloat16 [8, 4096, 5120], P('dp', 'ctx'), may hold values from -6 to 6
- value_weight: bfloat16 [5120, 512], replicated, may hold values from -0.078125 to 0.078125
- queries: bfloat16 [8, 4096, 2560], P('dp', 'ctx'), may hold values from -8 to 8
- keys: bfloat16 [8, 4096, 512], P('dp', 'ctx'), may hold values from -8 to 8
- out_grad: bfloat16 [8, 4096, 2560], P('dp', 'ctx'), may hold values from -6 to 6
Outputs:
- attended: bfloat16 [8, 4096, 2560], P('dp', 'ctx')
- query_grad: float32 [8, 4096, 2560], P('dp', 'ctx')
- key_grad: float32 [8, 4096, 512], P('dp', 'ctx')
- value_grad: float32 [8, 4096, 512], P('dp', 'ctx')
- weight_grad: float32 [5120, 512], P('ctx')
All inputs are finite; a program needn't handle non-finite values.
Results may differ from a plain program's by a relative error of at most 0.028.
Values may be sent and summed in bfloat16 or wider, within the bound.
A program may use at most 192 MiB of HBM per device.

v0:
```python
import math

import jax
import jax.numpy as jnp
from jax import lax
from jax.sharding import PartitionSpec as P

HEAD = 128


neg_floor = -1e30


def masked_scores(query_rows, key_step, allowed, score_scale):
    scores = (
        jnp.einsum("tgeh,sgh->gets", query_rows, key_step, preferred_element_type=jnp.float32)
        * score_scale
    )
    return jnp.where(allowed[None, None], scores, -jnp.inf)


def stats_block(state, query_rows, key_step, allowed, score_scale):
    masked = masked_scores(query_rows, key_step, allowed, score_scale)
    row_top = jnp.maximum(state[0], jnp.max(masked, axis=-1))
    row_total = state[1] * jnp.exp(state[0] - row_top) + jnp.sum(
        jnp.exp(masked - row_top[..., None]), axis=-1
    )
    return (row_top, row_total)


def attend_block(accum, query_rows, key_step, value_step, allowed, log_total, score_scale):
    masked = masked_scores(query_rows, key_step, allowed, score_scale)
    weights = jnp.exp(masked - log_total[..., None]).astype(jnp.bfloat16)
    return accum + jnp.einsum(
        "gets,sgh->geth", weights, value_step, preferred_element_type=jnp.float32
    )


def backward_block(
    query_rows, grad_rows, log_total, row_delta, key_step, value_step, allowed, score_scale
):
    masked = masked_scores(query_rows, key_step, allowed, score_scale)
    prob_full = jnp.exp(masked - log_total[..., None])
    weights = prob_full.astype(jnp.bfloat16)
    prob_grad = jnp.einsum(
        "tgeh,sgh->gets", grad_rows, value_step, preferred_element_type=jnp.float32
    )
    score_grad = (prob_full * (prob_grad - row_delta[..., None]) * score_scale).astype(jnp.bfloat16)
    query_part = jnp.einsum(
        "gets,sgh->tgeh", score_grad, key_step, preferred_element_type=jnp.float32
    )
    key_part = jnp.einsum(
        "gets,tgeh->sgh", score_grad, query_rows, preferred_element_type=jnp.float32
    )
    value_part = jnp.einsum(
        "gets,tgeh->sgh", weights, grad_rows, preferred_element_type=jnp.float32
    )
    return (query_part, key_part, value_part)


def per_device(hidden_in, value_weight, queries, keys, out_grad):
    tok_rows = queries.shape[1]
    kv_width = keys.shape[2]
    heads_kv = kv_width // HEAD
    group_size = queries.shape[2] // kv_width
    rank_count = lax.axis_size("ctx")
    my_rank = lax.axis_index("ctx")
    score_scale = 1.0 / math.sqrt(HEAD)
    seq_rows = rank_count * tok_rows
    step_rows = math.gcd(seq_rows, 512)
    step_count = seq_rows // step_rows
    help_rows = rank_count // 4 * tok_rows
    help_span = -(-help_rows // step_rows) * step_rows
    hidden_rows = hidden_in[0]
    query_rows = queries[0].reshape(tok_rows, heads_kv, group_size, HEAD)
    grad_rows = out_grad[0].reshape(tok_rows, heads_kv, group_size, HEAD)
    values = jnp.dot(hidden_rows, value_weight, preferred_element_type=jnp.float32).astype(
        jnp.bfloat16
    )
    joined = jnp.concatenate([keys[0], values], axis=1)
    every_kv = lax.all_gather(joined, "ctx", axis=0, tiled=True)
    query_pos = my_rank * tok_rows + jnp.arange(tok_rows, dtype=jnp.int32)
    last_own = my_rank * tok_rows + tok_rows - 1
    own_low = jnp.zeros((), jnp.int32)
    helping = jnp.zeros((), jnp.bool_)

    def pick_keys(key_start):
        kv_piece = lax.dynamic_slice_in_dim(every_kv, key_start, step_rows, 0)
        key_step = kv_piece[:, :kv_width].reshape(step_rows, heads_kv, HEAD)
        value_step = kv_piece[:, kv_width:].reshape(step_rows, heads_kv, HEAD)
        return (key_step, value_step)

    def step_masks(key_start):
        key_pos = key_start + jnp.arange(step_rows, dtype=jnp.int32)
        own_allowed = (key_pos[None, :] <= query_pos[:, None]) & (key_pos[None, :] >= own_low)
        own_needed = (key_start <= last_own) & (key_start + step_rows > own_low)
        help_allowed = jnp.broadcast_to(key_pos[None, :] < help_rows, (tok_rows, step_rows))
        help_needed = helping & (key_start < help_rows)
        return (own_allowed, own_needed, help_allowed, help_needed)

    def fresh_stats():
        return (
            jnp.full((heads_kv, group_size, tok_rows), neg_floor, jnp.float32),
            jnp.zeros((heads_kv, group_size, tok_rows), jnp.float32),
        )

    def stats_turn(turn_index, states):
        own_state, help_state = states
        key_start = turn_index * step_rows
        key_step, value_step = pick_keys(key_start)
        own_allowed, own_needed, help_allowed, help_needed = step_masks(key_start)
        own_state = lax.cond(
            own_needed,
            lambda state: stats_block(state, query_rows, key_step, own_allowed, score_scale),
            lambda state: state,
            own_state,
        )
        help_state = lax.cond(
            help_needed,
            lambda state: stats_block(state, query_rows, key_step, help_allowed, score_scale),
            lambda state: state,
            help_state,
        )
        return (own_state, help_state)

    own_state, help_state = lax.fori_loop(0, step_count, stats_turn, (fresh_stats(), fresh_stats()))
    log_total = own_state[0] + jnp.log(own_state[1])

    def attend_turn(turn_index, accums):
        own_acc, help_acc = accums
        key_start = turn_index * step_rows
        key_step, value_step = pick_keys(key_start)
        own_allowed, own_needed, help_allowed, help_needed = step_masks(key_start)
        own_acc = lax.cond(
            own_needed,
            lambda accum: attend_block(
                accum, query_rows, key_step, value_step, own_allowed, log_total, score_scale
            ),
            lambda accum: accum,
            own_acc,
        )
        help_acc = lax.cond(
            help_needed,
            lambda accum: attend_block(
                accum, query_rows, key_step, value_step, help_allowed, log_total, score_scale
            ),
            lambda accum: accum,
            help_acc,
        )
        return (own_acc, help_acc)

    acc_zero = jnp.zeros((heads_kv, group_size, tok_rows, HEAD), jnp.float32)
    own_acc, help_acc = lax.fori_loop(0, step_count, attend_turn, (acc_zero, acc_zero))
    attended_heads = own_acc.astype(jnp.bfloat16)
    attended_rows = attended_heads.transpose(2, 0, 1, 3)
    row_delta = jnp.sum(
        grad_rows.astype(jnp.float32) * attended_rows.astype(jnp.float32), axis=-1
    ).transpose(1, 2, 0)

    def backward_turn(turn_index, carried):
        own_buffers, help_buffers = carried
        key_start = turn_index * step_rows
        key_step, value_step = pick_keys(key_start)
        own_allowed, own_needed, help_allowed, help_needed = step_masks(key_start)

        def own_work(buffers):
            query_part, key_part, value_part = backward_block(
                query_rows,
                grad_rows,
                log_total,
                row_delta,
                key_step,
                value_step,
                own_allowed,
                score_scale,
            )
            term_block = jnp.concatenate(
                [key_part.reshape(step_rows, kv_width), value_part.reshape(step_rows, kv_width)],
                axis=1,
            )
            return (
                buffers[0] + query_part,
                lax.dynamic_update_slice_in_dim(buffers[1], term_block, key_start, 0),
            )

        def help_work(buffers):
            query_part, key_part, value_part = backward_block(
                query_rows,
                grad_rows,
                log_total,
                row_delta,
                key_step,
                value_step,
                help_allowed,
                score_scale,
            )
            term_block = jnp.concatenate(
                [key_part.reshape(step_rows, kv_width), value_part.reshape(step_rows, kv_width)],
                axis=1,
            )
            return (
                buffers[0] + query_part,
                lax.dynamic_update_slice_in_dim(buffers[1], term_block, key_start, 0),
            )

        own_buffers = lax.cond(own_needed, own_work, lambda buffers: buffers, own_buffers)
        help_buffers = lax.cond(help_needed, help_work, lambda buffers: buffers, help_buffers)
        return (own_buffers, help_buffers)

    query_zero = jnp.zeros((tok_rows, heads_kv, group_size, HEAD), jnp.float32)
    own_init = (query_zero, jnp.zeros((seq_rows, 2 * kv_width), jnp.float32))
    help_init = (query_zero, jnp.zeros((help_span, 2 * kv_width), jnp.float32))
    own_buffers, help_buffers = lax.fori_loop(0, step_count, backward_turn, (own_init, help_init))
    own_query, own_terms = own_buffers
    query_grad = own_query.reshape(tok_rows, heads_kv * group_size * HEAD)
    summed = lax.psum_scatter(
        own_terms.astype(jnp.bfloat16), "ctx", scatter_dimension=0, tiled=True
    ).astype(jnp.float32)
    key_grad = summed[:, :kv_width]
    value_grad = summed[:, kv_width:]
    value_grad_round = value_grad.astype(jnp.bfloat16)
    block_sum = lax.psum_scatter(
        lax.dot_general(
            hidden_rows,
            value_grad_round,
            (((0,), (0,)), ((), ())),
            preferred_element_type=jnp.float32,
        ).astype(jnp.bfloat16),
        "ctx",
        scatter_dimension=0,
        tiled=True,
    ).astype(jnp.float32)
    grad_sum = lax.psum(block_sum, "dp")
    weight_grad = grad_sum / math.sqrt(lax.axis_size("dp") * seq_rows)
    attended = attended_rows.reshape(tok_rows, heads_kv * group_size * HEAD)
    return (attended[None], query_grad[None], key_grad[None], value_grad[None], weight_grad)


def solution(mesh):
    return jax.shard_map(
        per_device,
        mesh=mesh,
        in_specs=(
            P("dp", "ctx", None),
            P(),
            P("dp", "ctx", None),
            P("dp", "ctx", None),
            P("dp", "ctx", None),
        ),
        out_specs=(
            P("dp", "ctx", None),
            P("dp", "ctx", None),
            P("dp", "ctx", None),
            P("dp", "ctx", None),
            P("ctx", None),
        ),
        check_vma=False,
    )
```

profile of v0, /device:TPU:2, one launch (start us, length us, event | category | flops | bytes accessed | tf_op | source)
XLA Modules:
  0.0 803.9 jit_solution(2913122942191882197)
XLA Ops:
  7.2 0.0 copy-start
  7.2 0.0 copy-start.8
  7.2 0.0 copy-start.6
  7.2 0.0 copy-start.7
  7.2 0.0 all-gather.2.cloned.1.call-start
  7.3 1.2 copy-done
  8.5 3.3 fusion.42
  11.8 0.0 copy-done.8
  11.8 0.7 pad_maximum_fusion
  12.6 0.0 all-gather.2.cloned.1.call-update
  12.6 0.0 reduce-scatter.5.cloned.1.call-start
  12.7 0.0 copy-done.6
  12.7 0.3 copy.83
  13.0 0.3 copy.87
  13.3 0.0 copy-done.7
  13.3 1.1 copy.89
  14.4 98.4 %all-gather.2.cloned.1.call-done = bf16[4096,1024]{1,0:T(8,128)(2,1)} async-done(((bf16[128,1024]{1,0:T(8,128)(2,1)}), bf16[4096,1024]{1,0:T(8,128)(2,1)}) %all-gather.2.cloned.1.call-update) | async-done | bytes 8388624 | tf_op jit(solution)/shard_map/all_gather | solution.py:81
  112.8 11.3 %copy.86 = bf16[4096,1024]{0,1:T(8,128)(2,1)} copy(bf16[4096,1024]{1,0:T(8,128)(2,1)} %all-gather.2.cloned.1.call-done) | data formatting | bytes 16777216
  124.1 4.0 while.49
  124.1 3.5 conditional.9
  124.2 0.2 compare_and_fusion
  124.4 1.1 constant_dynamic-slice_fusion
  125.5 1.0 fusion.6
  126.5 1.1 exponential_reduce_fusion
  128.1 1.2 broadcast_in_dim.83
  129.3 7.5 while.50
  129.3 7.1 conditional.10
  129.4 0.2 compare_and_fusion.1
  129.6 2.1 constant_dynamic-slice_fusion.1
  131.6 4.7 fusion.18
  136.8 1.6 copy.88
  138.5 0.0 copy-start.1
  138.5 1.5 multiply_reduce_fusion
  140.0 0.0 copy-done.1
  140.0 0.1 broadcast_in_dim.86
  140.2 4.3 broadcast_in_dim.87
  144.4 9.7 %while.51 = (s32[]{:T(128)}, f32[128,4,5,128]{3,0,2,1:T(8,128)S(1)}, bf16[4096,1024]{0,1:T(8,128)(2,1)}, s32[]{:T(128)}, bf16[4096,1024]{0,1:T(8,128)(2,1)}, /*i...) while((s32[]{:T(128)}, ...), condition=%wide.region_14.15_spmd.clone, body=%wide.region_11.14_spmd.clone.sunk | while | flops 1694696576 | bytes 38512008 | solution.py:213
  144.5 9.3 %conditional.11 = ((f32[128,4,5,128]{3,0,2,1:T(8,128)S(1)}, bf16[4096,1024]{0,1:T(8,128)(2,1)})) conditional(s32[]{:T(128)} %convert_element_type.96, (f32[128,4,5,128]{3,0,2,1:T(8,128)S(1)}, bf16[4096,1024]{0,1:T(8,128)(2,1)}) %tuple.155, (s32[]{:T(128)}, s32[1,512]{1,0:T(1,128)S(1)}, s32[]{:T(128)}, bf16[4096,1024]{0,1:T(8,128)(2,1)}, ...), branch_computations={%region_12.12_spmd, %region_13.13_spmd} | conditional | flops 1694696576 | bytes 38509172 | solution.py:206
  144.5 0.2 compare_and_fusion.2
  144.7 1.3 fusion.45
  146.0 0.9 fusion.46
  146.9 1.4 fusion.29
  148.3 1.9 fusion.25
  150.2 1.0 fusion.47
  151.2 1.4 fusion.35
  152.6 1.1 maximum_dynamic-update-slice_fusion
  154.1 12.0 %copy.92 = bf16[4096,1024]{1,0:T(8,128)(2,1)} copy(bf16[4096,1024]{0,1:T(8,128)(2,1)} %get-tuple-element.690) | data formatting | bytes 16777216 | tf_op jit(solution)/shard_map/while | solution.py:213
  166.2 0.0 reduce-scatter.5.cloned.1.call-update
  166.2 0.0 reduce-scatter.7.cloned.1.call-start
  166.2 363.2 %reduce-scatter.5.cloned.1.call-done = bf16[128,1024]{1,0:T(8,128)(2,1)} async-done(((bf16[4096,1024]{1,0:T(8,128)(2,1)}), bf16[128,1024]{1,0:T(8,128)(2,1)}) %reduce-scatter.5.cloned.1.call-update) | async-done | bytes 262160 | tf_op jit(solution)/shard_map/reduce_scatter | solution.py:216
  529.4 1.0 convert_element_type.68
  530.4 3.9 fusion.38
  534.3 7.9 copy.122
  542.2 0.0 reduce-scatter.7.cloned.1.call-update
  542.3 1.1 copy-done.2
  543.3 1.1 copy.93
  544.4 1.5 copy.91
  545.9 2.8 copy.94
  548.7 0.0 copy-done.4
  548.7 0.8 slice_bitcast_fusion.1
  549.5 216.7 %reduce-scatter.7.cloned.1.call-done = bf16[160,512]{1,0:T(8,128)(2,1)} async-done(((bf16[5120,512]{1,0:T(8,128)(2,1)}), bf16[160,512]{1,0:T(8,128)(2,1)}) %reduce-scatter.7.cloned.1.call-update) | async-done | bytes 163856
  766.2 1.0 copy.123
  767.2 29.1 %all-reduce.1 = f32[160,512]{0,1:T(8,128)S(1)} all-reduce(bf16[160,512]{0,1:T(8,128)(2,1)S(1)} %copy.123), channel_id=1, replica_groups=mesh['dp'=8,'ctx'=32] {'dp'}, use_global_device_ids=true, to_apply=%region_17.18 | all-reduce | flops 81920 | bytes 491520 | tf_op jit(solution)/shard_map/psum | solution.py:233
  796.5 0.9 copy.95
  (88 shorter events, 0.6 us)
Async XLA Ops:
  7.2 1.3 copy-start
  7.2 4.7 copy-start.8
  7.2 5.5 copy-start.6
  7.2 6.1 copy-start.7
  7.2 105.6 %all-gather.2.cloned.1.call-start = ((), (), s32[]{:S(2)}) async-start(), calls=%async_computation.2 | async-start | bytes 8650752 | tf_op jit(solution)/shard_map/all_gather | solution.py:81
  12.6 516.8 %reduce-scatter.5.cloned.1.call-start = ((), (), s32[]{:S(2)}) async-start(), calls=%async_computation.3 | async-start | bytes 8650752 | tf_op jit(solution)/shard_map/reduce_scatter | solution.py:216
  138.5 1.6 copy-start.1
  144.5 2.4 copy-start.5
  166.2 600.0 %reduce-scatter.7.cloned.1.call-start = ((), (), s32[]{:S(2)}) async-start(), calls=%async_computation.4 | async-start | bytes 5406720
  530.4 3.9 copy-start.3
  542.2 1.1 copy-start.2
  544.4 4.3 copy-start.4
Sparse Core Ops, SparseCore 0:
  12.7 100.0 all-gather.1
  166.3 363.0 reduce-scatter.4
  542.4 223.7 reduce-scatter.6
where the time goes:
time: 806 us; the launch traced here: 804 us
  waiting for transfers between devices  678 us (84%)
  local copies, waits for them, and re-layouts  55.3 us (7%)
  blocking collectives  29.1 us (4%)
  matrix products  19.6 us (2%)
  between operations  13.9 us (2%)
    reduce_scatter x1, waiting for transfers between devices, per_device(): lax.psum_scatter(own_terms.astype(jnp.bfloat16), 'ctx', scatter_dimension...  363 us
    unnamed x4, waiting for transfers between devices  217 us
    all_gather x1, waiting for transfers between devices, per_device(): every_kv = lax.all_gather(joined, 'ctx', axis=0, tiled=True)  98.4 us
    psum x1, blocking collectives, per_device(): grad_sum = lax.psum(block_sum, 'dp')  29.1 us
    unnamed x25, local copies, waits for them, and re-layouts  29.1 us
  transfers between devices with their start and end apart: 3, of which 3 were waited for; matrix products, arithmetic and copies ran while one was open for 1% of the time, Pallas kernels for 0%

commit v1 on v0

v1 whole, which is shorter than its diff:
```python
import math

import jax
import jax.numpy as jnp
from jax import lax
from jax.experimental import pallas as pl
from jax.experimental.pallas import tpu as pltpu
from jax.sharding import PartitionSpec as P

BF = jnp.bfloat16
F32 = jnp.float32
SCALE = 1.0 / math.sqrt(128.0)
C2 = math.log2(math.e) * SCALE
NEG = -1e30
NX, NZ, NDP = 4, 8, 8
TOK = 128
BLK = NX * TOK
GROUP = 5
HEAD = 128
QG = GROUP * HEAD
WIDTH = 5120
ROWS = 160
PAD = 192
YROWS = PAD // 4
KCHUNKS = 4
UPS, DNS = 4, 3


def dot(a, b):
    return jnp.dot(a, b, preferred_element_type=F32)


def lanes(start, size):
    return pl.ds(pl.multiple_of(start, 128), size)


def rows(start, size):
    return pl.ds(pl.multiple_of(start, 16), size)


def kernel(
    hid_in, vw_in, q_in, k_in, do_in,
    att_out, dq_out, dk_out, dv_out, w_out,
    hid, vw, vals, qbuf, dobuf, kbuf, vbuf, ktbuf, qt, dot_t, pbuf, mhist, mrun, lrun, delta, ot, dqt,
    o_own, dq_own, dq_all, hid_t, hid_r,
    vs, vr, ks, kr, dv_own, dk_own, dv_all, dk_all,
    w_sib, w_sib_r, w_own, w_y, w_yr, w_z, w_zr, w_f, w_all,
    lsem, qsem, ksem, vsem, osem, hsem, asem, dqsem, gvsem, gksem, ksem_r, vsem_r, rvsem, rksem,
    csem, ysem, zsem, fsem,
):
    dp = lax.axis_index("dp")
    ctx = lax.axis_index("ctx")
    z, x = ctx // NX, ctx % NX
    y, c = dp // 2, dp % 2

    def at_x(d):
        return (dp, z * NX + (x + d) % NX)

    def at_z(d):
        return (dp, ((z + d) % NZ) * NX + x)

    def at_dp(d):
        return ((dp + d) % NDP, ctx)

    def remote(src, dst, sems, slot, device):
        return pltpu.make_async_remote_copy(
            src_ref=src, dst_ref=dst, send_sem=sems.at[0, slot], recv_sem=sems.at[1, slot],
            device_id=device, device_id_type=pl.DeviceIdType.MESH,
        )

    def wait_recv(dst, sems, slot):
        remote(dst, dst, sems, slot, at_x(1)).wait_recv()

    hid_copy = pltpu.make_async_copy(hid_in, hid, lsem.at[0])
    hid_copy.start()
    step_k = WIDTH // KCHUNKS
    vw_copies = []
    for i in range(KCHUNKS):
        part = pl.ds(i * step_k, step_k)
        vw_copies.append(pltpu.make_async_copy(vw_in.at[part], vw.at[part], lsem.at[1 + i]))
        vw_copies[-1].start()
    mine = rows(x * TOK, TOK)
    own_q = pltpu.make_async_copy(q_in.at[:, lanes(x * QG, QG)], qbuf.at[mine], lsem.at[5])
    own_k = pltpu.make_async_copy(k_in.at[:, lanes(x * HEAD, HEAD)], kbuf.at[z, mine], lsem.at[6])
    own_do = pltpu.make_async_copy(do_in.at[:, lanes(x * QG, QG)], dobuf.at[mine], lsem.at[7])
    own_q.start()
    own_k.start()
    own_do.start()

    barrier = pltpu.get_barrier_semaphore()
    partners = [at_x(d) for d in range(1, NX)] + [at_z(d) for d in range(1, NZ)]
    partners += [at_dp(d) for d in range(1, NDP)]
    for device in partners:
        pl.semaphore_signal(barrier, inc=1, device_id=device, device_id_type=pl.DeviceIdType.MESH)
    pl.semaphore_wait(barrier, len(partners))

    def exchange(source, target, sems):
        copies = []
        for d in range(1, NX):
            copies.append(remote(source((x + d) % NX), target(x), sems, d - 1, at_x(d)))
            copies[-1].start()
        return copies

    def arrive(target, sems):
        for d in range(1, NX):
            wait_recv(target((x + NX - d) % NX), sems, d - 1)

    sent = []
    to_k = lambda src: kbuf.at[z, rows(src * TOK, TOK)]
    to_v = lambda src: vbuf.at[z, rows(src * TOK, TOK)]
    to_q = lambda src: qbuf.at[rows(src * TOK, TOK)]
    to_do = lambda src: dobuf.at[rows(src * TOK, TOK)]
    to_hid = lambda src: hid_r.at[:, :, lanes(src * TOK, TOK)]
    sent += exchange(lambda dst: k_in.at[:, lanes(dst * HEAD, HEAD)], to_k, ksem)
    sent += exchange(lambda dst: q_in.at[:, lanes(dst * QG, QG)], to_q, qsem)

    hid_copy.wait()
    total = None
    for i in range(KCHUNKS):
        vw_copies[i].wait()
        part = slice(i * step_k, (i + 1) * step_k)
        term = dot(hid[:, part], vw[part, :])
        total = term if total is None else total + term
    vals[...] = total.astype(BF)
    vbuf[z, mine, :] = vals[:, lanes(x * HEAD, HEAD)]
    sent += exchange(lambda dst: vals.at[:, lanes(dst * HEAD, HEAD)], to_v, vsem)
    sent += exchange(lambda dst: do_in.at[:, lanes(dst * QG, QG)], to_do, osem)

    def ring(buf, sems, up, step):
        block = z - step + 1 if up else (z + step - 1) % NZ
        valid = (block >= 0) & (z < NZ - 1) if up else block < DNS
        slot = step - 1 if up else UPS + step - 1
        return block, valid, remote(
            buf.at[lax.rem(block + NZ, NZ)], buf.at[lax.rem(block + NZ, NZ)], sems, slot, at_z(1 if up else NZ - 1)
        )

    def ring_send(buf, sems, up, step):
        _, valid, copy = ring(buf, sems, up, step)
        pl.when(valid)(lambda: copy.start())

    def ring_sent(buf, sems, up, step):
        _, valid, copy = ring(buf, sems, up, step)
        pl.when(valid)(lambda: copy.wait_send())

    own_k.wait()
    arrive(to_k, ksem)
    ring_send(kbuf, ksem_r, True, 1)
    ring_send(kbuf, ksem_r, False, 1)
    for i in range(NZ):
        flipped = hid[:, i * 640:(i + 1) * 640].T
        for j in range(NX):
            hid_t[j, i] = flipped[j * ROWS:(j + 1) * ROWS]
    arrive(to_v, vsem)
    ring_send(vbuf, vsem_r, True, 1)
    ring_send(vbuf, vsem_r, False, 1)
    own_q.wait()
    arrive(to_q, qsem)
    sent += exchange(lambda dst: hid_t.at[dst], to_hid, hsem)
    own_hid = pltpu.make_async_copy(hid_t.at[x], to_hid(x), lsem.at[8])
    own_hid.start()

    for h in range(GROUP):
        qt[h] = qbuf[:, h * HEAD:(h + 1) * HEAD].T
    mrun[...] = jnp.full_like(mrun, NEG)
    lrun[...] = jnp.zeros_like(lrun)
    ot[...] = jnp.zeros_like(ot)
    dqt[...] = jnp.zeros_like(dqt)

    def forward(block, diagonal):
        k = kbuf[block]
        ktbuf[block] = k.T
        v_t = vbuf[block].T
        if diagonal:
            allowed = lax.broadcasted_iota(jnp.int32, (BLK, BLK), 0) <= lax.broadcasted_iota(
                jnp.int32, (BLK, BLK), 1
            )
        for h in range(GROUP):
            s = dot(k, qt[h])
            if diagonal:
                s = jnp.where(allowed, s, NEG)
            m_old = mrun[h]
            m_new = jnp.maximum(m_old, jnp.max(s, axis=0, keepdims=True))
            p = jnp.exp2((s - m_new) * C2)
            shrink = jnp.exp2((m_old - m_new) * C2)
            lrun[h] = lrun[h] * shrink + jnp.sum(p, axis=0, keepdims=True)
            p_round = p.astype(BF)
            pbuf[block * GROUP + h] = p_round
            mhist[block * GROUP + h] = m_new
            mrun[h] = m_new
            ot[h] = ot[h] * shrink + dot(v_t, p_round)

    forward(z, True)

    def forward_step(step, carry):
        up_block = z - step
        down_block = (z + step) % NZ
        up_valid = up_block >= 0
        down_valid = (down_block < DNS) & (step <= DNS)

        @pl.when(up_valid)
        def _():
            wait_recv(kbuf.at[up_block], ksem_r, step - 1)

            @pl.when((step < UPS) & (z < NZ - 1))
            def _():
                ring_send(kbuf, ksem_r, True, step + 1)

        @pl.when(down_valid)
        def _():
            wait_recv(kbuf.at[down_block], ksem_r, UPS + step - 1)

            @pl.when(step < DNS)
            def _():
                ring_send(kbuf, ksem_r, False, step + 1)

        @pl.when(up_valid)
        def _():
            wait_recv(vbuf.at[up_block], vsem_r, step - 1)

            @pl.when((step < UPS) & (z < NZ - 1))
            def _():
                ring_send(vbuf, vsem_r, True, step + 1)

        @pl.when(down_valid)
        def _():
            wait_recv(vbuf.at[down_block], vsem_r, UPS + step - 1)

            @pl.when(step < DNS)
            def _():
                ring_send(vbuf, vsem_r, False, step + 1)

        @pl.when(up_valid)
        def _():
            forward(up_block, False)

        @pl.when(down_valid & (down_block < z))
        def _():
            forward(down_block, False)

        return carry

    lax.fori_loop(1, UPS + 1, forward_step, 0)

    own_do.wait()
    arrive(to_do, osem)
    for h in range(GROUP):
        part = slice(h * HEAD, (h + 1) * HEAD)
        dot_t[h] = dobuf[:, part].T
        inverse = 1.0 / lrun[h]
        o = (ot[h] * inverse).astype(BF)
        o_own[:, part] = o.T
        delta[h] = jnp.sum(o.astype(F32) * dot_t[h].astype(F32), axis=0, keepdims=True)
        lrun[h] = inverse
    to_att = lambda src: att_out.at[:, lanes(src * QG, QG)]
    sent += exchange(lambda dst: o_own.at[rows(dst * TOK, TOK)], to_att, asem)
    own_att = pltpu.make_async_copy(o_own.at[mine], to_att(x), lsem.at[9])
    own_att.start()

    def grad_copy(send, recv, sems, slot, up):
        return remote(send.at[slot], recv.at[slot], sems, slot, at_z(1 if up else NZ - 1))

    def reduce_step(step, term, send, recv, sems):
        down_block = z - 5 + step
        up_block = (z + 4 - step) % NZ

        @pl.when(down_block >= 0)
        def _():
            own = term(down_block)
            slot = step - 1
            chained = (step >= 2) & (z < NZ - 1)

            @pl.when(chained)
            def _():
                wait_recv(recv.at[step - 2], sems, step - 2)
                send[slot] = (own + recv[step - 2].astype(F32)).astype(BF)

            @pl.when(jnp.logical_not(chained))
            def _():
                send[slot] = own.astype(BF)

            grad_copy(send, recv, sems, slot, False).start()

        up_valid = (step <= DNS) & (up_block < DNS)

        @pl.when(up_valid)
        def _():
            slot = UPS + step - 1

            @pl.when(step >= 2)
            def _():
                wait_recv(recv.at[slot - 1], sems, slot - 1)

            @pl.when(up_block < z)
            def _():
                own = term(up_block)

                @pl.when(step >= 2)
                def _():
                    send[slot] = (own + recv[slot - 1].astype(F32)).astype(BF)

                @pl.when(step < 2)
                def _():
                    send[slot] = own.astype(BF)

            @pl.when(up_block >= z)
            def _():
                send[slot] = recv[slot - 1]

            grad_copy(send, recv, sems, slot, True).start()

    def reduce_last(own, target, recv, sems):
        acc[...] = own

        @pl.when(z < NZ - 1)
        def _():
            wait_recv(recv.at[UPS - 1], sems, UPS - 1)
            acc[...] += recv[UPS - 1].astype(F32)

        @pl.when(z < DNS)
        def _():
            wait_recv(recv.at[UPS + DNS - 1], sems, UPS + DNS - 1)
            acc[...] += recv[UPS + DNS - 1].astype(F32)

        target[...] = acc[...].astype(BF)

    def reduce_sent(send, recv, sems):
        for step in range(1, UPS + 1):
            pl.when(z - 5 + step >= 0)(
                lambda: grad_copy(send, recv, sems, step - 1, False).wait_send()
            )
        for step in range(1, DNS + 1):
            pl.when((z + 4 - step) % NZ < DNS)(
                lambda: grad_copy(send, recv, sems, UPS + step - 1, True).wait_send()
            )

    acc = w_own.at[pl.ds(0, BLK), pl.ds(0, HEAD)]

    def value_term(block):
        total = None
        for h in range(GROUP):
            at = block * GROUP + h
            factor = jnp.exp2((mhist[at] - mrun[h]) * C2) * lrun[h]
            p = (pbuf[at].astype(F32) * factor).astype(BF)
            pbuf[at] = p
            term = dot(p, dobuf[:, h * HEAD:(h + 1) * HEAD])
            total = term if total is None else total + term
        return total

    def key_term(block):
        v = vbuf[block]
        k_t = ktbuf[block]
        total = None
        for h in range(GROUP):
            dp_t = dot(v, dot_t[h])
            ds = (pbuf[block * GROUP + h].astype(F32) * (dp_t - delta[h])).astype(BF)
            dqt[h] += dot(k_t, ds)
            term = dot(ds, qbuf[:, h * HEAD:(h + 1) * HEAD])
            total = term if total is None else total + term
        return total * SCALE

    def value_step(step, carry):
        reduce_step(step, value_term, vs, vr, rvsem)
        return carry

    lax.fori_loop(1, UPS + 1, value_step, 0)
    reduce_last(value_term(z), dv_own, vr, rvsem)
    to_dv = lambda src: dv_all.at[:, lanes(src * HEAD, HEAD)]
    sent += exchange(lambda dst: dv_own, to_dv, gvsem)
    dv_all[:, lanes(x * HEAD, HEAD)] = dv_own[...]

    far = lanes((1 - c) * 256, 256)
    near = lanes(c * 256, 256)
    sibling = (y * 2 + 1 - c, ctx)
    core_copy = remote(w_sib, w_sib_r, csem, 0, sibling)

    def stage_product():
        arrive(to_dv, gvsem)
        own_hid.wait()
        arrive(to_hid, hsem)
        dv_out[...] = dv_all[mine, :].astype(F32)

        def far_part(i, carry):
            at = rows(i * 320, 320)
            h2 = hid_r[pl.ds(i * 2, 2)].reshape(320, BLK)
            w_sib[at, :] = dot(h2, dv_all[:, far]).astype(BF)
            return carry

        def near_part(i, carry):
            at = rows(i * 320, 320)
            h2 = hid_r[pl.ds(i * 2, 2)].reshape(320, BLK)
            w_own[at, :] = dot(h2, dv_all[:, near])
            return carry

        lax.fori_loop(0, 4, far_part, 0)
        core_copy.start()
        lax.fori_loop(0, 4, near_part, 0)

    def y_copy(d):
        to = (y + d) % 4
        device = (to * 2 + c, ctx)
        return remote(w_y.at[:, rows(to * YROWS, YROWS)], w_yr.at[d - 1], ysem, d - 1, device)

    def stage_y():
        core_copy.wait_recv()
        for i in range(NZ):
            part = slice(i * ROWS, (i + 1) * ROWS)
            w_y[i, :ROWS] = (w_own[part, :] + w_sib_r[part, :].astype(F32)).astype(BF)
        w_y[:, ROWS:] = jnp.zeros((NZ, PAD - ROWS, 256), BF)
        for d in range(1, 4):
            y_copy(d).start()

    def z_copy(d):
        to = (z + d) % NZ
        return remote(w_z.at[to], w_zr.at[d - 1], zsem, d - 1, at_z(d))

    def stage_z():
        for d in range(1, 4):
            wait_recv(w_yr.at[d - 1], ysem, d - 1)
        total = w_y[:, rows(y * YROWS, YROWS), :].astype(F32)
        for d in range(1, 4):
            total += w_yr[d - 1].astype(F32)
        w_z[...] = total.astype(BF)
        for d in range(1, NZ):
            z_copy(d).start()

    def f_copy(d):
        return remote(w_f, w_all.at[c, rows(y * YROWS, YROWS)], fsem, d - 1, at_dp(d))

    def stage_f():
        for d in range(1, NZ):
            wait_recv(w_zr.at[d - 1], zsem, d - 1)
        total = w_z[z].astype(F32)
        for d in range(1, NZ):
            total += w_zr[d - 1].astype(F32)
        w_f[...] = (total * (1.0 / math.sqrt(32768.0))).astype(BF)
        w_all[c, rows(y * YROWS, YROWS), :] = w_f[...]
        for d in range(1, NDP):
            f_copy(d).start()

    def key_step(step, carry):
        reduce_step(step, key_term, ks, kr, rksem)
        pl.when(step == 1)(stage_product)
        pl.when(step == 2)(stage_y)
        pl.when(step == 3)(stage_z)
        pl.when(step == 4)(stage_f)
        return carry

    lax.fori_loop(1, UPS + 1, key_step, 0)
    last = key_term(z)
    for h in range(GROUP):
        dq_own[:, h * HEAD:(h + 1) * HEAD] = (dqt[h] * SCALE).astype(BF).T
    to_dq = lambda src: dq_all.at[:, lanes(src * QG, QG)]
    sent += exchange(lambda dst: dq_own.at[rows(dst * TOK, TOK)], to_dq, dqsem)
    dq_all[:, lanes(x * QG, QG)] = dq_own[mine, :]
    reduce_last(last, dk_own, kr, rksem)
    to_dk = lambda src: dk_all.at[:, lanes(src * HEAD, HEAD)]
    sent += exchange(lambda dst: dk_own.at[rows(dst * TOK, TOK)], to_dk, gksem)
    dk_all[:, lanes(x * HEAD, HEAD)] = dk_own[mine, :]

    for d in range(1, NDP):
        src = (dp + NDP - d) % NDP
        wait_recv(w_all.at[src % 2, rows(src // 2 * YROWS, YROWS)], fsem, d - 1)
    w_out[:, :256] = w_all[0, :ROWS].astype(F32)
    w_out[:, 256:] = w_all[1, :ROWS].astype(F32)
    arrive(to_dk, gksem)
    dk_out[...] = dk_all[...].astype(F32)
    arrive(to_dq, dqsem)
    dq_out[...] = dq_all[...].astype(F32)
    own_att.wait()
    arrive(to_att, asem)

    for copy in sent:
        copy.wait_send()
    for buf, sems in ((kbuf, ksem_r), (vbuf, vsem_r)):
        for step in range(1, UPS + 1):
            ring_sent(buf, sems, True, step)
        for step in range(1, DNS + 1):
            ring_sent(buf, sems, False, step)
    reduce_sent(vs, vr, rvsem)
    reduce_sent(ks, kr, rksem)
    core_copy.wait_send()
    for d in range(1, 4):
        y_copy(d).wait_send()
    for d in range(1, NZ):
        z_copy(d).wait_send()
    for d in range(1, NDP):
        f_copy(d).wait_send()


def per_device(hidden_in, value_weight, queries, keys, out_grad):
    vmem = pl.BlockSpec(memory_space=pltpu.VMEM)
    anywhere = pl.BlockSpec(memory_space=pl.ANY)
    dma = pltpu.SemaphoreType.DMA
    att, dq, dk, dv, w = pl.pallas_call(
        kernel,
        out_shape=[
            jax.ShapeDtypeStruct((TOK, 2560), BF),
            jax.ShapeDtypeStruct((TOK, 2560), F32),
            jax.ShapeDtypeStruct((TOK, 512), F32),
            jax.ShapeDtypeStruct((TOK, 512), F32),
            jax.ShapeDtypeStruct((ROWS, 512), F32),
        ],
        in_specs=[anywhere] * 5,
        out_specs=[anywhere, vmem, vmem, vmem, vmem],
        scratch_shapes=[
            pltpu.VMEM((TOK, WIDTH), BF),
            pltpu.VMEM((WIDTH, 512), BF),
            pltpu.VMEM((TOK, 512), BF),
            pltpu.VMEM((BLK, QG), BF),
            pltpu.VMEM((BLK, QG), BF),
            pltpu.VMEM((NZ, BLK, HEAD), BF),
            pltpu.VMEM((NZ, BLK, HEAD), BF),
            pltpu.VMEM((NZ, HEAD, BLK), BF),
            pltpu.VMEM((GROUP, HEAD, BLK), BF),
            pltpu.VMEM((GROUP, HEAD, BLK), BF),
            pltpu.VMEM((NZ * GROUP, BLK, BLK), BF),
            pltpu.VMEM((NZ * GROUP, 1, BLK), F32),
            pltpu.VMEM((GROUP, 1, BLK), F32),
            pltpu.VMEM((GROUP, 1, BLK), F32),
            pltpu.VMEM((GROUP, 1, BLK), F32),
            pltpu.VMEM((GROUP, HEAD, BLK), F32),
            pltpu.VMEM((GROUP, HEAD, BLK), F32),
            pltpu.VMEM((BLK, QG), BF),
            pltpu.VMEM((BLK, QG), BF),
            pltpu.VMEM((TOK, 2560), BF),
            pltpu.VMEM((NX, NZ, ROWS, TOK), BF),
            pltpu.VMEM((NZ, ROWS, BLK), BF),
            pltpu.VMEM((UPS + DNS, BLK, HEAD), BF),
            pltpu.VMEM((UPS + DNS, BLK, HEAD), BF),
            pltpu.VMEM((UPS + DNS, BLK, HEAD), BF),
            pltpu.VMEM((UPS + DNS, BLK, HEAD), BF),
            pltpu.VMEM((BLK, HEAD), BF),
            pltpu.VMEM((BLK, HEAD), BF),
            pltpu.VMEM((BLK, 512), BF),
            pltpu.VMEM((TOK, 512), BF),
            pltpu.VMEM((NZ * ROWS, 256), BF),
            pltpu.VMEM((NZ * ROWS, 256), BF),
            pltpu.VMEM((NZ * ROWS, 256), F32),
            pltpu.VMEM((NZ, PAD, 256), BF),
            pltpu.VMEM((3, NZ, YROWS, 256), BF),
            pltpu.VMEM((NZ, YROWS, 256), BF),
            pltpu.VMEM((NZ - 1, YROWS, 256), BF),
            pltpu.VMEM((YROWS, 256), BF),
            pltpu.VMEM((2, PAD, 256), BF),
            dma((10,)),
            dma((2, 3)),
            dma((2, 3)),
            dma((2, 3)),
            dma((2, 3)),
            dma((2, 3)),
            dma((2, 3)),
            dma((2, 3)),
            dma((2, 3)),
            dma((2, 3)),
            dma((2, UPS + DNS)),
            dma((2, UPS + DNS)),
            dma((2, UPS + DNS)),
            dma((2, UPS + DNS)),
            dma((2, 1)),
            dma((2, 3)),
            dma((2, NZ - 1)),
            dma((2, NDP - 1)),
        ],
        compiler_params=pltpu.CompilerParams(
            collective_id=0, has_side_effects=True, vmem_limit_bytes=60 * 2**20
        ),
    )(hidden_in[0], value_weight, queries[0], keys[0], out_grad[0])
    return (att[None], dq[None], dk[None], dv[None], w)


def solution(mesh):
    return jax.shard_map(
        per_device,
        mesh=mesh,
        in_specs=(
            P("dp", "ctx", None),
            P(),
            P("dp", "ctx", None),
            P("dp", "ctx", None),
            P("dp", "ctx", None),
        ),
        out_specs=(
            P("dp", "ctx", None),
            P("dp", "ctx", None),
            P("dp", "ctx", None),
            P("dp", "ctx", None),
            P("ctx", None),
        ),
        check_vma=False,
    )
```

time: 806 us -> 117 us (0.15)
  waiting for transfers between devices: 678 us -> 0 us
  Pallas kernels: 0 us -> 110 us
  local copies, waits for them, and re-layouts: 55.3 us -> 5.27 us
  blocking collectives: 29.1 us -> 0 us
  matrix products: 19.6 us -> 0 us
  between operations: 13.9 us -> 0.66 us
    reduce_scatter x1 -> x0, waiting for transfers between devices: 363 us -> none  [per_device(): lax.psum_scatter(own_terms.astype(jnp.bfloat16), 'ctx', scatter_dimension...]
    unnamed x4 -> x0, waiting for transfers between devices: 217 us -> none
    pallas_call x0 -> x1, Pallas kernels: none -> 110 us  [per_device(): pl.pallas_call(kernel, out_shape=[jax.ShapeDtypeStruct((TOK, 2560), BF),...]
    all_gather x1 -> x0, waiting for transfers between devices: 98.4 us -> none  [per_device(): every_kv = lax.all_gather(joined, 'ctx', axis=0, tiled=True)]
    psum x1 -> x0, blocking collectives: 29.1 us -> none  [per_device(): grad_sum = lax.psum(block_sum, 'dp')]
    unnamed x25 -> x13, local copies, waits for them, and re-layouts: 29.1 us -> 5.27 us
    dot_general x9 -> x0, matrix products: 19.6 us -> none  [the longest x1 4.74 us: attend_block(): jnp.einsum('gets,sgh->geth', weights, value_step, preferred_element_type=...]
    while x3 -> x0, local copies, waits for them, and re-layouts: 15.2 us -> none  [the longest x2 13.5 us: per_device(): lax.fori_loop(0, step_count, backward_turn, (own_init, help_init))]
  transfers between devices with their start and end apart: 3 -> 0, of which waited for: 3 -> 0; matrix products, arithmetic and copies ran while one was open for 1% -> 0% of each run, Pallas kernels for 0% -> 0%
where the time goes in v1:
time: 117 us; the launch traced here: 116 us
  Pallas kernels  110 us (94%)
  local copies, waits for them, and re-layouts  5.27 us (5%)
    pallas_call x1, Pallas kernels, per_device(): pl.pallas_call(kernel, out_shape=[jax.ShapeDtypeStruct((TOK, 2560), BF),...  110 us
    unnamed x13, local copies, waits for them, and re-layouts  5.27 us

profile of v1, /device:TPU:2, one launch (start us, length us, event | category | flops | bytes accessed | tf_op | source)
XLA Modules:
  0.0 115.7 jit_solution(11839994710240999522)
XLA Ops:
  0.6 109.8 %shard_map.92 = (bf16[128,2560]{1,0:T(8,128)(2,1)}, f32[128,2560]{1,0:T(8,128)}, f32[128,512]{1,0:T(8,128)}, f32[128,512]{1,0:T(8,128)}, f32[160,512]{1,0:T(8,128)}) custom-call(bf16[128,5120]{1,0:T(8,128)(2,1)} %bitcast.9, bf16[5120,512]{1,0:T(8,128)(2,1)} %vw_in.1, bf16[128,2560]{1,0:T(8,128)(2,1)} %bitcast.11, bf16[128,512]{1,0:T(8,128)(2,1)} %bitcast.15, ...), custom_call_target="tpu_custom_call" | custom-call | tf_op jit(solution)/shard_map/pallas_call | solution.py:494
  110.4 0.0 copy-start
  110.4 2.1 %copy.15 = bf16[1,128,2560]{2,1,0:T(8,128)(2,1)} copy(bf16[1,128,2560]{2,1,0:T(8,128)(2,1)} %bitcast.10) | data formatting | bytes 1310720
  112.5 0.0 copy-done
  112.5 0.0 copy-start.3
  112.5 0.0 copy-start.2
  112.5 0.0 copy-start.1
  112.5 1.1 copy.16
  113.5 0.0 copy-done.3
  113.5 0.7 copy.17
  114.3 0.0 copy-done.2
  114.3 0.7 copy.18
  115.0 0.0 copy-done.1
  115.0 0.7 copy.19
Async XLA Ops:
  110.4 2.1 %copy-start = (f32[128,2560]{1,0:T(8,128)S(1)}, f32[128,2560]{1,0:T(8,128)}, u32[]{:S(2)}) copy-start(f32[128,2560]{1,0:T(8,128)} %get-tuple-element.11) | copy-start | bytes 3932164
  112.5 1.1 copy-start.3
  112.5 1.8 %copy-start.2 = (f32[128,512]{1,0:T(8,128)S(1)}, f32[128,512]{1,0:T(8,128)}, u32[]{:S(2)}) copy-start(f32[128,512]{1,0:T(8,128)} %get-tuple-element.13) | copy-start | bytes 786436
  112.5 2.5 %copy-start.1 = (f32[160,512]{1,0:T(8,128)S(1)}, f32[160,512]{1,0:T(8,128)}, u32[]{:S(2)}) copy-start(f32[160,512]{1,0:T(8,128)} %get-tuple-element.24) | copy-start | bytes 983044

commit v2 on v1

v2 whole, which is shorter than its diff:
```python
import math

import jax
import jax.numpy as jnp
from jax import lax
from jax.experimental import pallas as pl
from jax.experimental.pallas import tpu as pltpu
from jax.sharding import PartitionSpec as P

BF = jnp.bfloat16
F32 = jnp.float32
SCALE = 1.0 / math.sqrt(128.0)
C2 = math.log2(math.e) * SCALE
NEG = -1e30
NX, NZ, NDP = 4, 8, 8
TOK = 128
BLK = NX * TOK
GROUP = 5
HEAD = 128
QG = GROUP * HEAD
WIDTH = 5120
ROWS = 160
PAD = 192
YROWS = PAD // 4
KCHUNKS = 4
STEPS = 4
K_HOPS, V_HOPS = (4, 3), (3, 4)
KEY_HOPS = ((4, 3),)
VALUE_HOPS = ((4, 3), (3, 4), (4, 3), (3, 4))
Q_FIRST = 256


def dot(a, b):
    return jnp.dot(a, b, preferred_element_type=F32)


def lanes(start, size):
    return pl.ds(pl.multiple_of(start, 128), size)


def rows(start, size):
    return pl.ds(pl.multiple_of(start, 16), size)


def kernel(
    hid_in, vw_in, q_in, k_in, do_in,
    att_out, dq_out, dk_out, dv_out, w_all,
    hid, vw, vals, qbuf, dobuf, kbuf, vbuf, ktbuf, qt, dot_t, pbuf, mhist, mrun, lrun, delta, ot, dqt,
    o_own, dq_own, hid_t, hid_r, acc,
    vs, vr, ks, kr, dv_own, dk_own, dv_all,
    w_y, w_yr, w_z, w_zr, w_f,
    lsem, qsem, ksem, vsem, osem, hsem, asem, dqsem, gvsem, gosem, gksem, ksem_r, vsem_r, rvsem, rksem,
    csem, ysem, zsem, fsem,
):
    dp = lax.axis_index("dp")
    ctx = lax.axis_index("ctx")
    z, x = ctx // NX, ctx % NX
    y, c = dp // 2, dp % 2

    def at_x(d):
        return (dp, z * NX + (x + d) % NX)

    def at_z(d):
        return (dp, ((z + d) % NZ) * NX + x)

    def at_dp(d):
        return ((dp + d) % NDP, ctx)

    def remote(src, dst, sems, slot, device):
        return pltpu.make_async_remote_copy(
            src_ref=src, dst_ref=dst, send_sem=sems.at[0, slot], recv_sem=sems.at[1, slot],
            device_id=device, device_id_type=pl.DeviceIdType.MESH,
        )

    def wait_recv(dst, sems, slot):
        remote(dst, dst, sems, slot, at_x(1)).wait_recv()

    hid_copy = pltpu.make_async_copy(hid_in, hid, lsem.at[0])
    hid_copy.start()
    step_k = WIDTH // KCHUNKS
    vw_copies = []
    for i in range(KCHUNKS):
        part = pl.ds(i * step_k, step_k)
        vw_copies.append(pltpu.make_async_copy(vw_in.at[part], vw.at[part], lsem.at[1 + i]))
        vw_copies[-1].start()
    mine = rows(x * TOK, TOK)
    own_q = pltpu.make_async_copy(q_in.at[:, lanes(x * QG, QG)], qbuf.at[mine], lsem.at[5])
    own_k = pltpu.make_async_copy(k_in.at[:, lanes(x * HEAD, HEAD)], kbuf.at[z, mine], lsem.at[6])
    own_do = pltpu.make_async_copy(do_in.at[:, lanes(x * QG, QG)], dobuf.at[mine], lsem.at[7])
    own_q.start()
    own_k.start()
    own_do.start()

    barrier = pltpu.get_barrier_semaphore()
    partners = [at_x(d) for d in range(1, NX)] + [at_z(d) for d in range(1, NZ)]
    partners += [at_dp(d) for d in range(1, NDP)]
    partners += [(y * 2 + 1 - c, z * NX + (x + d) % NX) for d in range(1, NX)]
    for device in partners:
        pl.semaphore_signal(barrier, inc=1, device_id=device, device_id_type=pl.DeviceIdType.MESH)
    pl.semaphore_wait(barrier, len(partners))

    def exchange(source, target, sems, first=0):
        copies = []
        for d in range(1, NX):
            copies.append(remote(source((x + d) % NX), target(x), sems, first + d - 1, at_x(d)))
            copies[-1].start()
        return copies

    def arrive(target, sems, first=0):
        for d in range(1, NX):
            wait_recv(target((x + NX - d) % NX), sems, first + d - 1)

    sent = []
    to_k = lambda src: kbuf.at[z, rows(src * TOK, TOK)]
    to_v = lambda src: vbuf.at[z, rows(src * TOK, TOK)]
    to_q = lambda src: qbuf.at[rows(src * TOK, TOK), pl.ds(0, Q_FIRST)]
    to_q2 = lambda src: qbuf.at[rows(src * TOK, TOK), pl.ds(Q_FIRST, QG - Q_FIRST)]
    to_do = lambda src: dobuf.at[rows(src * TOK, TOK)]
    to_hid = lambda src: hid_r.at[:, :, lanes(c * BLK + src * TOK, TOK)]
    sent += exchange(lambda dst: k_in.at[:, lanes(dst * HEAD, HEAD)], to_k, ksem)
    sent += exchange(lambda dst: q_in.at[:, lanes(dst * QG, Q_FIRST)], to_q, qsem)

    def ring_send(buf, sems, hops, up, step, act=lambda copy: copy.start()):
        block = z - step + 1 if up else (z + step - 1) % NZ
        valid = (block >= 0) & (z < NZ - 1) if up else block < hops[1]
        slot = step - 1 if up else hops[0] + step - 1
        at = buf.at[(block + NZ) % NZ]
        pl.when(valid)(lambda: act(remote(at, at, sems, slot, at_z(1 if up else NZ - 1))))

    def ring_first(buf, sems, hops):
        ring_send(buf, sems, hops, True, 1)
        ring_send(buf, sems, hops, False, 1)

    hid_copy.wait()
    for i in range(NZ):
        flipped = hid[:, i * 640:(i + 1) * 640].T
        for j in range(NX):
            hid_t[j, i] = flipped[j * ROWS:(j + 1) * ROWS]
    for copy in vw_copies:
        copy.wait()
    vals[...] = dot(hid[...], vw[...]).astype(BF)
    vbuf[z, mine, :] = vals[:, lanes(x * HEAD, HEAD)]
    sent += exchange(lambda dst: vals.at[:, lanes(dst * HEAD, HEAD)], to_v, vsem)
    sent += exchange(
        lambda dst: q_in.at[:, lanes(dst * QG + Q_FIRST, QG - Q_FIRST)], to_q2, qsem, 3
    )
    own_k.wait()
    arrive(to_k, ksem)
    ring_first(kbuf, ksem_r, K_HOPS)
    arrive(to_v, vsem)
    ring_first(vbuf, vsem_r, V_HOPS)
    sent += exchange(lambda dst: do_in.at[:, lanes(dst * QG, QG)], to_do, osem)
    own_q.wait()
    arrive(to_q, qsem)
    arrive(to_q2, qsem, 3)
    sent += exchange(lambda dst: hid_t.at[dst], to_hid, hsem)
    own_hid = pltpu.make_async_copy(hid_t.at[x], to_hid(x), lsem.at[8])
    own_hid.start()

    for h in range(GROUP):
        qt[h] = qbuf[:, h * HEAD:(h + 1) * HEAD].T
    mrun[...] = jnp.full_like(mrun, NEG)
    lrun[...] = jnp.zeros_like(lrun)
    ot[...] = jnp.zeros_like(ot)
    dqt[...] = jnp.zeros_like(dqt)

    def forward(block, diagonal):
        k = kbuf[block]
        ktbuf[block] = k.T
        v_t = jnp.concatenate([vbuf[block].T, jnp.ones((16, BLK), BF)], axis=0)
        if diagonal:
            allowed = lax.broadcasted_iota(jnp.int32, (BLK, BLK), 0) <= lax.broadcasted_iota(
                jnp.int32, (BLK, BLK), 1
            )

        def weigh(h, s):
            if diagonal:
                s = jnp.where(allowed, s, NEG)
            m_old = mrun[h]
            m_new = jnp.maximum(m_old, jnp.max(s, axis=0, keepdims=True))
            shift = m_new * C2
            p = jnp.exp2(s * C2 - shift).astype(BF)
            pbuf[block * GROUP + h] = p
            mhist[block * GROUP + h] = m_new
            mrun[h] = m_new
            return p, jnp.exp2(m_old * C2 - shift)

        def gather(h, p, shrink):
            o = dot(v_t, p)
            ot[h] = ot[h] * shrink + o[:HEAD]
            lrun[h] = lrun[h] * shrink + o[HEAD:HEAD + 1]

        s = dot(k, qt[0])
        held = None
        for h in range(GROUP):
            s_next = dot(k, qt[h + 1]) if h + 1 < GROUP else None
            if held is not None:
                gather(*held)
            held = (h, *weigh(h, s))
            s = s_next
        gather(*held)

    def pass_on(buf, sems, hops, step):
        ups, dns = hops

        @pl.when((z - step >= 0) & (step <= ups))
        def _():
            wait_recv(buf.at[(z - step + NZ) % NZ], sems, step - 1)
            pl.when(step < ups)(lambda: ring_send(buf, sems, hops, True, step + 1))

        @pl.when(((z + step) % NZ < dns) & (step <= dns))
        def _():
            wait_recv(buf.at[(z + step) % NZ], sems, ups + step - 1)
            pl.when(step < dns)(lambda: ring_send(buf, sems, hops, False, step + 1))

    pass_on(kbuf, ksem_r, K_HOPS, 1)
    forward(z, True)
    pass_on(vbuf, vsem_r, V_HOPS, 1)

    def forward_step(step, carry):
        below = (z + step) % NZ
        pl.when(z - step >= 0)(lambda: forward((z - step + NZ) % NZ, False))
        pass_on(kbuf, ksem_r, K_HOPS, step + 1)
        pl.when((step < STEPS) & (below < NZ - 1 - STEPS) & (below < z))(lambda: forward(below, False))
        pass_on(vbuf, vsem_r, V_HOPS, step + 1)
        return carry

    lax.fori_loop(1, STEPS + 1, forward_step, 0)

    own_do.wait()
    arrive(to_do, osem)
    for h in range(GROUP):
        part = slice(h * HEAD, (h + 1) * HEAD)
        dot_t[h] = dobuf[:, part].T
        inverse = 1.0 / lrun[h]
        o = (ot[h] * inverse).astype(BF)
        o_own[:, part] = o.T
        delta[h] = jnp.sum(o.astype(F32) * dot_t[h].astype(F32), axis=0, keepdims=True)
        lrun[h] = inverse
    to_att = lambda src: att_out.at[:, lanes(src * QG, QG)]
    sent += exchange(lambda dst: o_own.at[rows(dst * TOK, TOK)], to_att, asem)
    own_att = pltpu.make_async_copy(o_own.at[mine], to_att(x), lsem.at[9])
    own_att.start()

    def hop_copy(send, recv, sems, up, slot, part, parts):
        at = pl.ds(part * (BLK // parts), BLK // parts)
        return remote(
            send.at[slot, at], recv.at[slot, at], sems, part * (NZ - 1) + slot, at_z(1 if up else NZ - 1)
        )

    def hop_plan(hops, step, up):
        ups = hops[1]
        if up:
            block = (z + ups + 1 - step) % NZ
            return block, (step <= ups) & (block < ups), hops[0] + step - 1
        block = z - hops[0] - 1 + step
        return (block + NZ) % NZ, (step <= hops[0]) & (block >= 0), step - 1

    def reduce_step(step, term, send, recv, sems, plan):
        parts = len(plan)
        size = BLK // parts
        for part in range(parts):
            at = pl.ds(part * size, size)
            for up in (False, True):
                block, valid, slot = hop_plan(plan[part], step, up)

                @pl.when(valid)
                def _():
                    if up:

                        @pl.when(block < z)
                        def _():
                            acc[:size] = term(block, part, parts)

                        @pl.when(block >= z)
                        def _():
                            acc[:size] = jnp.zeros((size, HEAD), F32)
                    else:
                        acc[:size] = term(block, part, parts)

                    @pl.when((step >= 2) if up else (step >= 2) & (z < NZ - 1))
                    def _():
                        wait_recv(recv.at[slot - 1, at], sems, part * (NZ - 1) + slot - 1)
                        acc[:size] += recv[slot - 1, at].astype(F32)

                    send[slot, at] = acc[:size].astype(BF)
                    hop_copy(send, recv, sems, up, slot, part, parts).start()

    def reduce_last(term, target, recv, sems, plan, done=lambda part, at: None):
        parts = len(plan)
        size = BLK // parts
        for part, (dns, ups) in enumerate(plan):
            at = pl.ds(part * size, size)
            acc[:size] = term(z, part, parts)
            for valid, slot in ((z < NZ - 1, dns - 1), (z < ups, dns + ups - 1)):

                @pl.when(valid)
                def _():
                    wait_recv(recv.at[slot, at], sems, part * (NZ - 1) + slot)
                    acc[:size] += recv[slot, at].astype(F32)

            target[at] = acc[:size].astype(BF)
            done(part, at)

    def reduce_sent(send, recv, sems, plan):
        for part in range(len(plan)):
            for up in (False, True):
                for step in range(1, STEPS + 1):
                    if step <= plan[part][1 if up else 0]:
                        _, valid, slot = hop_plan(plan[part], step, up)
                        pl.when(valid)(
                            lambda: hop_copy(send, recv, sems, up, slot, part, len(plan)).wait_send()
                        )

    def value_term(block, part=0, parts=1):
        keys = pl.ds(part * (BLK // parts), BLK // parts)
        total = None
        for h in range(GROUP):
            at = block * GROUP + h
            factor = jnp.exp2((mhist[at] - mrun[h]) * C2) * lrun[h]
            p = (pbuf[at, keys].astype(F32) * factor).astype(BF)
            pbuf[at, keys] = p
            term = dot(p, dobuf[:, h * HEAD:(h + 1) * HEAD])
            total = term if total is None else total + term
        return total

    def key_term(block, part=0, parts=1):
        v = vbuf[block]
        k_t = ktbuf[block]
        total = None
        dp_next = dot(v, dot_t[0])
        for h in range(GROUP):
            dp_t = dp_next
            dp_next = dot(v, dot_t[h + 1]) if h + 1 < GROUP else None
            ds = (pbuf[block * GROUP + h].astype(F32) * (dp_t - delta[h])).astype(BF)
            dqt[h] += dot(k_t, ds)
            term = dot(ds, qbuf[:, h * HEAD:(h + 1) * HEAD])
            total = term if total is None else total + term
        return total * SCALE

    def value_step(step, carry):
        reduce_step(step, value_term, vs, vr, rvsem, VALUE_HOPS)
        return carry

    lax.fori_loop(1, STEPS + 1, value_step, 0)
    own_hid.wait()
    arrive(to_hid, hsem)
    sibling = (y * 2 + 1 - c, ctx)
    hid_half = hid_r.at[:, :, lanes(c * BLK, BLK)]
    hid_copy2 = remote(hid_half, hid_half, csem, 0, sibling)
    hid_copy2.start()

    def share(part, d):
        at = pl.ds(part * (BLK // len(VALUE_HOPS)), BLK // len(VALUE_HOPS))
        slot = (part * 2 + x % 2) * 2 + c
        return pltpu.make_async_remote_copy(
            src_ref=dv_own.at[at],
            dst_ref=dv_all.at[c, at, lanes(x % 2 * HEAD, HEAD)],
            send_sem=gvsem.at[0, part * NX + d],
            recv_sem=gvsem.at[1, slot],
            device_id=(y * 2 + x // 2, z * NX + (x + d) % NX),
            device_id_type=pl.DeviceIdType.MESH,
        )

    def share_all(part, at):
        for d in range(1, NX):
            share(part, d).start()
        pl.when(x // 2 != c)(lambda: share(part, 0).start())

        @pl.when(x // 2 == c)
        def _():
            dv_all[c, at, lanes(x % 2 * HEAD, HEAD)] = dv_own[at]

    reduce_last(value_term, dv_own, vr, rvsem, VALUE_HOPS, share_all)
    to_dv = lambda src: dv_out.at[:, lanes(src * HEAD, HEAD)]
    sent += exchange(lambda dst: dv_own.at[rows(dst * TOK, TOK)], to_dv, gosem)
    dv_out[:, lanes(x * HEAD, HEAD)] = dv_own[mine, :]

    halves = (0, 1)

    def y_copy(i, d):
        to = (y + d) % 4
        return remote(
            w_y.at[i, :, rows(to * YROWS, YROWS)], w_yr.at[i, d - 1], ysem, i * 3 + d - 1, (to * 2 + c, ctx)
        )

    def stage_product():
        hid_copy2.wait_recv()
        for part in range(len(VALUE_HOPS)):
            at = pl.ds(part * (BLK // len(VALUE_HOPS)), BLK // len(VALUE_HOPS))
            for j in (0, 1):
                for core in (0, 1):

                    @pl.when((x != c * 2 + j) | (c != core))
                    def _():
                        wait_recv(dv_all.at[core, at, pl.ds(j * HEAD, HEAD)], gvsem, (part * 2 + j) * 2 + core)

        w_y[:, :, ROWS:] = jnp.zeros((2, NZ, PAD - ROWS, HEAD), BF)
        h_rows = hid_r[...].reshape(NZ * ROWS, 2 * BLK)
        total = dot(h_rows, dv_all[...].reshape(2 * BLK, 256)).astype(BF)
        for i in halves:
            w_y[i, :, :ROWS] = total[:, i * HEAD:(i + 1) * HEAD].reshape(NZ, ROWS, HEAD)
            for d in range(1, 4):
                y_copy(i, d).start()

    def z_copy(i, d):
        return remote(w_z.at[i, (z + d) % NZ], w_zr.at[i, d - 1], zsem, i * (NZ - 1) + d - 1, at_z(d))

    def stage_z():
        for i in halves:
            total = w_y[i, :, rows(y * YROWS, YROWS), :].astype(F32)
            for d in range(1, 4):
                wait_recv(w_yr.at[i, d - 1], ysem, i * 3 + d - 1)
                total += w_yr[i, d - 1].astype(F32)
            w_z[i] = total.astype(BF)
            for d in range(1, NZ):
                z_copy(i, d).start()

    def f_copy(i, d):
        target = w_all.at[c * 2 + i, rows(y * YROWS, YROWS)]
        return remote(w_f.at[i], target, fsem, i * (NDP - 1) + d - 1, at_dp(d))

    def stage_f():
        for i in halves:
            total = w_z[i, z].astype(F32)
            for d in range(1, NZ):
                wait_recv(w_zr.at[i, d - 1], zsem, i * (NZ - 1) + d - 1)
                total += w_zr[i, d - 1].astype(F32)
            w_f[i] = (total * (1.0 / math.sqrt(32768.0))).astype(BF)
            w_all[c * 2 + i, rows(y * YROWS, YROWS), :] = w_f[i]
            for d in range(1, NDP):
                f_copy(i, d).start()

    def key_step(step, carry):
        reduce_step(step, key_term, ks, kr, rksem, KEY_HOPS)
        pl.when(step == 1)(stage_product)
        return carry

    lax.fori_loop(1, STEPS + 1, key_step, 0)
    last = key_term(z)
    for h in range(GROUP):
        dq_own[:, h * HEAD:(h + 1) * HEAD] = (dqt[h] * SCALE).astype(BF).T
    to_dq = lambda src: dq_out.at[:, lanes(src * QG, QG)]
    sent += exchange(lambda dst: dq_own.at[rows(dst * TOK, TOK)], to_dq, dqsem)
    own_dq = pltpu.make_async_copy(dq_own.at[mine], to_dq(x), lsem.at[0])
    own_dq.start()
    stage_z()
    reduce_last(lambda block, part, parts: last, dk_own, kr, rksem, KEY_HOPS)
    to_dk = lambda src: dk_out.at[:, lanes(src * HEAD, HEAD)]
    sent += exchange(lambda dst: dk_own.at[rows(dst * TOK, TOK)], to_dk, gksem)
    dk_out[:, lanes(x * HEAD, HEAD)] = dk_own[mine, :]
    stage_f()

    own_dq.wait()
    own_att.wait()
    arrive(to_att, asem)
    for copy in sent:
        copy.wait_send()
    for buf, sems, hops in ((kbuf, ksem_r, K_HOPS), (vbuf, vsem_r, V_HOPS)):
        for up in (True, False):
            for step in range(1, hops[0 if up else 1] + 1):
                ring_send(buf, sems, hops, up, step, lambda copy: copy.wait_send())
    reduce_sent(vs, vr, rvsem, VALUE_HOPS)
    reduce_sent(ks, kr, rksem, KEY_HOPS)
    for i in halves:
        for d in range(1, 4):
            y_copy(i, d).wait_send()
        for d in range(1, NZ):
            z_copy(i, d).wait_send()
    hid_copy2.wait_send()
    for part in range(len(VALUE_HOPS)):
        for d in range(1, NX):
            share(part, d).wait_send()
        pl.when(x // 2 != c)(lambda: share(part, 0).wait_send())
    arrive(to_dv, gosem)
    arrive(to_dk, gksem)
    arrive(to_dq, dqsem)
    for i in halves:
        for d in range(1, NDP):
            src = (dp + NDP - d) % NDP
            target = w_all.at[src % 2 * 2 + i, rows(src // 2 * YROWS, YROWS)]
            wait_recv(target, fsem, i * (NDP - 1) + d - 1)
            f_copy(i, d).wait_send()


def finish(att, dq, dk, dv, w, att_out, dq_out, dk_out, dv_out, w_out):
    att_out[...] = att[...]
    dq_out[...] = dq[...].astype(F32)
    dk_out[...] = dk[...].astype(F32)
    dv_out[...] = dv[...].astype(F32)
    for i in range(4):
        w_out[:, i * HEAD:(i + 1) * HEAD] = w[i, :ROWS].astype(F32)


def per_device(hidden_in, value_weight, queries, keys, out_grad):
    vmem = pl.BlockSpec(memory_space=pltpu.VMEM)
    anywhere = pl.BlockSpec(memory_space=pl.ANY)
    dma = pltpu.SemaphoreType.DMA
    parts = pl.pallas_call(
        kernel,
        out_shape=[
            jax.ShapeDtypeStruct((TOK, 2560), BF),
            jax.ShapeDtypeStruct((TOK, 2560), BF),
            jax.ShapeDtypeStruct((TOK, 512), BF),
            jax.ShapeDtypeStruct((TOK, 512), BF),
            jax.ShapeDtypeStruct((4, PAD, HEAD), BF),
        ],
        in_specs=[anywhere] * 5,
        out_specs=[anywhere, anywhere, vmem, vmem, vmem],
        scratch_shapes=[
            pltpu.VMEM((TOK, WIDTH), BF),
            pltpu.VMEM((WIDTH, 512), BF),
            pltpu.VMEM((TOK, 512), BF),
            pltpu.VMEM((BLK, QG), BF),
            pltpu.VMEM((BLK, QG), BF),
            pltpu.VMEM((NZ, BLK, HEAD), BF),
            pltpu.VMEM((NZ, BLK, HEAD), BF),
            pltpu.VMEM((NZ, HEAD, BLK), BF),
            pltpu.VMEM((GROUP, HEAD, BLK), BF),
            pltpu.VMEM((GROUP, HEAD, BLK), BF),
            pltpu.VMEM((NZ * GROUP, BLK, BLK), BF),
            pltpu.VMEM((NZ * GROUP, 1, BLK), F32),
            pltpu.VMEM((GROUP, 1, BLK), F32),
            pltpu.VMEM((GROUP, 1, BLK), F32),
            pltpu.VMEM((GROUP, 1, BLK), F32),
            pltpu.VMEM((GROUP, HEAD, BLK), F32),
            pltpu.VMEM((GROUP, HEAD, BLK), F32),
            pltpu.VMEM((BLK, QG), BF),
            pltpu.VMEM((BLK, QG), BF),
            pltpu.VMEM((NX, NZ, ROWS, TOK), BF),
            pltpu.VMEM((NZ, ROWS, 2 * BLK), BF),
            pltpu.VMEM((BLK, HEAD), F32),
            pltpu.VMEM((NZ - 1, BLK, HEAD), BF),
            pltpu.VMEM((NZ - 1, BLK, HEAD), BF),
            pltpu.VMEM((NZ - 1, BLK, HEAD), BF),
            pltpu.VMEM((NZ - 1, BLK, HEAD), BF),
            pltpu.VMEM((BLK, HEAD), BF),
            pltpu.VMEM((BLK, HEAD), BF),
            pltpu.VMEM((2, BLK, 256), BF),
            pltpu.VMEM((2, NZ, PAD, HEAD), BF),
            pltpu.VMEM((2, 3, NZ, YROWS, HEAD), BF),
            pltpu.VMEM((2, NZ, YROWS, HEAD), BF),
            pltpu.VMEM((2, NZ - 1, YROWS, HEAD), BF),
            pltpu.VMEM((2, YROWS, HEAD), BF),
            dma((10,)),
            dma((2, 6)),
            dma((2, 3)),
            dma((2, 3)),
            dma((2, 3)),
            dma((2, 3)),
            dma((2, 3)),
            dma((2, 3)),
            dma((2, 16)),
            dma((2, 3)),
            dma((2, 3)),
            dma((2, NZ - 1)),
            dma((2, NZ - 1)),
            dma((2, 4 * (NZ - 1))),
            dma((2, NZ - 1)),
            dma((2, 1)),
            dma((2, 6)),
            dma((2, 2 * (NZ - 1))),
            dma((2, 2 * (NDP - 1))),
        ],
        compiler_params=pltpu.CompilerParams(
            collective_id=0, has_side_effects=True, vmem_limit_bytes=60 * 2**20
        ),
    )(hidden_in[0], value_weight, queries[0], keys[0], out_grad[0])
    att, dq, dk, dv, w = pl.pallas_call(
        finish,
        out_shape=[
            jax.ShapeDtypeStruct((TOK, 2560), BF),
            jax.ShapeDtypeStruct((TOK, 2560), F32),
            jax.ShapeDtypeStruct((TOK, 512), F32),
            jax.ShapeDtypeStruct((TOK, 512), F32),
            jax.ShapeDtypeStruct((ROWS, 512), F32),
        ],
        in_specs=[vmem] * 5,
        out_specs=[vmem] * 5,
    )(*parts)
    return (att[None], dq[None], dk[None], dv[None], w)


def solution(mesh):
    return jax.shard_map(
        per_device,
        mesh=mesh,
        in_specs=(
            P("dp", "ctx", None),
            P(),
            P("dp", "ctx", None),
            P("dp", "ctx", None),
            P("dp", "ctx", None),
        ),
        out_specs=(
            P("dp", "ctx", None),
            P("dp", "ctx", None),
            P("dp", "ctx", None),
            P("dp", "ctx", None),
            P("ctx", None),
        ),
        check_vma=False,
    )
```

time: 117 us -> 95.5 us (0.82)
  Pallas kernels: 110 us -> 93.5 us
  local copies, waits for them, and re-layouts: 5.27 us -> 0 us
    pallas_call x1, Pallas kernels: 110 us -> 90.5 us  [per_device(): pl.pallas_call(kernel, out_shape=[jax.ShapeDtypeStruct((TOK, 2560), BF),...]
    unnamed x13 -> x0, local copies, waits for them, and re-layouts: 5.27 us -> none
    pallas_call x0 -> x1, Pallas kernels: none -> 3.05 us  [per_device(): pl.pallas_call(finish, out_shape=[jax.ShapeDtypeStruct((TOK, 2560), BF),...]
where the time goes in v2:
time: 95.5 us; the launch traced here: 94.2 us
  Pallas kernels  93.5 us (98%)
    pallas_call x1, Pallas kernels, per_device(): pl.pallas_call(kernel, out_shape=[jax.ShapeDtypeStruct((TOK, 2560), BF),...  90.5 us
    pallas_call x1, Pallas kernels, per_device(): pl.pallas_call(finish, out_shape=[jax.ShapeDtypeStruct((TOK, 2560), BF),...  3.05 us

profile of v2, /device:TPU:2, one launch (start us, length us, event | category | flops | bytes accessed | tf_op | source)
XLA Modules:
  0.0 94.2 jit_solution(4909131084211255459)
XLA Ops:
  0.6 90.5 %shard_map.92 = (bf16[128,2560]{1,0:T(8,128)(2,1)}, bf16[128,2560]{1,0:T(8,128)(2,1)}, bf16[128,512]{1,0:T(8,128)(2,1)}, bf16[128,512]{1,0:T(8,128)(2,1)}, bf16[4,192,128]{2,1,0:T(8,128)(2,1)}) custom-call(bf16[128,5120]{1,0:T(8,128)(2,1)} %bitcast.8, bf16[5120,512]{1,0:T(8,128)(2,1)} %vw_in.1, bf16[128,2560]{1,0:T(8,128)(2,1)} %bitcast.9, ...), custom_call_target="tpu_custom_call" | custom-call | tf_op jit(solution)/shard_map/pallas_call | solution.py:499
  91.1 3.0 %shard_map.93 = (bf16[128,2560]{1,0:T(8,128)(2,1)}, f32[128,2560]{1,0:T(8,128)}, f32[128,512]{1,0:T(8,128)}, f32[128,512]{1,0:T(8,128)}, f32[160,512]{1,0:T(8,128)}) custom-call(bf16[128,2560]{1,0:T(8,128)(2,1)} %get-tuple-element.15.att, bf16[128,2560]{1,0:T(8,128)(2,1)} %get-tuple-element.16.dq, bf16[128,512]{1,0:T(8,128)(2,1)} %get-tuple-element.17.dk, ...), custom_call_target="tpu_custom_call" | custom-call | tf_op jit(solution)/shard_map/pallas_call | solution.py:569

commit v3 on v2

--- a/solution.py
+++ b/solution.py
@@ -20,12 +20,11 @@
 QG = GROUP * HEAD
 WIDTH = 5120
 ROWS = 160
-PAD = 192
-YROWS = PAD // 4
+YROWS, YLESS = 48, 32
 KCHUNKS = 4
 STEPS = 4
-K_HOPS, V_HOPS = (4, 3), (3, 4)
-KEY_HOPS = ((4, 3),)
+K_HOPS, V_HOPS = (4, 3, 1), (3, 4, 2)
+KEY_HOPS = ((4, 3), (3, 4))
 VALUE_HOPS = ((4, 3), (3, 4), (4, 3), (3, 4))
 Q_FIRST = 256
 
@@ -120,22 +119,23 @@
     sent += exchange(lambda dst: k_in.at[:, lanes(dst * HEAD, HEAD)], to_k, ksem)
     sent += exchange(lambda dst: q_in.at[:, lanes(dst * QG, Q_FIRST)], to_q, qsem)
 
-    def ring_send(buf, sems, hops, up, step, act=lambda copy: copy.start()):
+    def ring_at(buf, block, part, parts):
+        return buf.at[(block + NZ) % NZ, pl.ds(part * (BLK // parts), BLK // parts)]
+
+    def ring_send(buf, sems, hops, up, step, part, act=lambda copy: copy.start()):
+        ups, dns, parts = hops
         block = z - step + 1 if up else (z + step - 1) % NZ
-        valid = (block >= 0) & (z < NZ - 1) if up else block < hops[1]
-        slot = step - 1 if up else hops[0] + step - 1
-        at = buf.at[(block + NZ) % NZ]
+        valid = (block >= 0) & (z < NZ - 1) if up else block < dns
+        slot = part * (NZ - 1) + (step - 1 if up else ups + step - 1)
+        at = ring_at(buf, block, part, parts)
         pl.when(valid)(lambda: act(remote(at, at, sems, slot, at_z(1 if up else NZ - 1))))
 
     def ring_first(buf, sems, hops):
-        ring_send(buf, sems, hops, True, 1)
-        ring_send(buf, sems, hops, False, 1)
+        for part in range(hops[2]):
+            ring_send(buf, sems, hops, True, 1, part)
+            ring_send(buf, sems, hops, False, 1, part)
 
     hid_copy.wait()
-    for i in range(NZ):
-        flipped = hid[:, i * 640:(i + 1) * 640].T
-        for j in range(NX):
-            hid_t[j, i] = flipped[j * ROWS:(j + 1) * ROWS]
     for copy in vw_copies:
         copy.wait()
     vals[...] = dot(hid[...], vw[...]).astype(BF)
@@ -144,27 +144,24 @@
     sent += exchange(
         lambda dst: q_in.at[:, lanes(dst * QG + Q_FIRST, QG - Q_FIRST)], to_q2, qsem, 3
     )
+    for i in range(NZ):
+        flipped = hid[:, i * 640:(i + 1) * 640].T
+        for j in range(NX):
+            hid_t[j, i] = flipped[j * ROWS:(j + 1) * ROWS]
     own_k.wait()
     arrive(to_k, ksem)
     ring_first(kbuf, ksem_r, K_HOPS)
     arrive(to_v, vsem)
     ring_first(vbuf, vsem_r, V_HOPS)
-    sent += exchange(lambda dst: do_in.at[:, lanes(dst * QG, QG)], to_do, osem)
     own_q.wait()
     arrive(to_q, qsem)
-    arrive(to_q2, qsem, 3)
-    sent += exchange(lambda dst: hid_t.at[dst], to_hid, hsem)
-    own_hid = pltpu.make_async_copy(hid_t.at[x], to_hid(x), lsem.at[8])
-    own_hid.start()
-
-    for h in range(GROUP):
-        qt[h] = qbuf[:, h * HEAD:(h + 1) * HEAD].T
+
     mrun[...] = jnp.full_like(mrun, NEG)
     lrun[...] = jnp.zeros_like(lrun)
     ot[...] = jnp.zeros_like(ot)
     dqt[...] = jnp.zeros_like(dqt)
 
-    def forward(block, diagonal):
+    def forward(block, diagonal, heads=tuple(range(GROUP))):
         k = kbuf[block]
         ktbuf[block] = k.T
         v_t = jnp.concatenate([vbuf[block].T, jnp.ones((16, BLK), BF)], axis=0)
@@ -190,10 +187,10 @@
             ot[h] = ot[h] * shrink + o[:HEAD]
             lrun[h] = lrun[h] * shrink + o[HEAD:HEAD + 1]
 
-        s = dot(k, qt[0])
+        s = dot(k, qt[heads[0]])
         held = None
-        for h in range(GROUP):
-            s_next = dot(k, qt[h + 1]) if h + 1 < GROUP else None
+        for h in heads:
+            s_next = dot(k, qt[h + 1]) if h < heads[-1] else None
             if held is not None:
                 gather(*held)
             held = (h, *weigh(h, s))
@@ -201,20 +198,33 @@
         gather(*held)
 
     def pass_on(buf, sems, hops, step):
-        ups, dns = hops
-
-        @pl.when((z - step >= 0) & (step <= ups))
-        def _():
-            wait_recv(buf.at[(z - step + NZ) % NZ], sems, step - 1)
-            pl.when(step < ups)(lambda: ring_send(buf, sems, hops, True, step + 1))
-
-        @pl.when(((z + step) % NZ < dns) & (step <= dns))
-        def _():
-            wait_recv(buf.at[(z + step) % NZ], sems, ups + step - 1)
-            pl.when(step < dns)(lambda: ring_send(buf, sems, hops, False, step + 1))
-
+        ups, dns, parts = hops
+        for part in range(parts):
+            first = part * (NZ - 1)
+
+            @pl.when((z - step >= 0) & (step <= ups))
+            def _():
+                wait_recv(ring_at(buf, z - step, part, parts), sems, first + step - 1)
+                pl.when(step < ups)(lambda: ring_send(buf, sems, hops, True, step + 1, part))
+
+            @pl.when(((z + step) % NZ < dns) & (step <= dns))
+            def _():
+                wait_recv(ring_at(buf, z + step, part, parts), sems, first + ups + step - 1)
+                pl.when(step < dns)(lambda: ring_send(buf, sems, hops, False, step + 1, part))
+
+    early = Q_FIRST // HEAD
+    for h in range(early):
+        qt[h] = qbuf[:, h * HEAD:(h + 1) * HEAD].T
+    forward(z, True, tuple(range(early)))
     pass_on(kbuf, ksem_r, K_HOPS, 1)
-    forward(z, True)
+    arrive(to_q2, qsem, 3)
+    sent += exchange(lambda dst: do_in.at[:, lanes(dst * QG, QG)], to_do, osem)
+    sent += exchange(lambda dst: hid_t.at[dst], to_hid, hsem)
+    own_hid = pltpu.make_async_copy(hid_t.at[x], to_hid(x), lsem.at[8])
+    own_hid.start()
+    for h in range(early, GROUP):
+        qt[h] = qbuf[:, h * HEAD:(h + 1) * HEAD].T
+    forward(z, True, tuple(range(early, GROUP)))
     pass_on(vbuf, vsem_r, V_HOPS, 1)
 
     def forward_step(step, carry):
@@ -230,17 +240,7 @@
     own_do.wait()
     arrive(to_do, osem)
     for h in range(GROUP):
-        part = slice(h * HEAD, (h + 1) * HEAD)
-        dot_t[h] = dobuf[:, part].T
-        inverse = 1.0 / lrun[h]
-        o = (ot[h] * inverse).astype(BF)
-        o_own[:, part] = o.T
-        delta[h] = jnp.sum(o.astype(F32) * dot_t[h].astype(F32), axis=0, keepdims=True)
-        lrun[h] = inverse
-    to_att = lambda src: att_out.at[:, lanes(src * QG, QG)]
-    sent += exchange(lambda dst: o_own.at[rows(dst * TOK, TOK)], to_att, asem)
-    own_att = pltpu.make_async_copy(o_own.at[mine], to_att(x), lsem.at[9])
-    own_att.start()
+        lrun[h] = 1.0 / lrun[h]
 
     def hop_copy(send, recv, sems, up, slot, part, parts):
         at = pl.ds(part * (BLK // parts), BLK // parts)
@@ -325,30 +325,49 @@
         return total
 
     def key_term(block, part=0, parts=1):
-        v = vbuf[block]
-        k_t = ktbuf[block]
+        keys = pl.ds(part * (BLK // parts), BLK // parts)
+        v = vbuf[block, keys]
+        k_t = ktbuf[block, :, pl.ds(part * (BLK // parts), BLK // parts)]
         total = None
         dp_next = dot(v, dot_t[0])
         for h in range(GROUP):
             dp_t = dp_next
             dp_next = dot(v, dot_t[h + 1]) if h + 1 < GROUP else None
-            ds = (pbuf[block * GROUP + h].astype(F32) * (dp_t - delta[h])).astype(BF)
+            ds = (pbuf[block * GROUP + h, keys].astype(F32) * (dp_t - delta[h])).astype(BF)
             dqt[h] += dot(k_t, ds)
             term = dot(ds, qbuf[:, h * HEAD:(h + 1) * HEAD])
             total = term if total is None else total + term
         return total * SCALE
 
+    to_att = lambda src: att_out.at[:, lanes(src * QG, QG)]
+    own_att = pltpu.make_async_copy(o_own.at[mine], to_att(x), lsem.at[9])
+
+    def att_copies():
+        return [
+            remote(o_own.at[rows((x + d) % NX * TOK, TOK)], to_att(x), asem, d - 1, at_x(d))
+            for d in range(1, NX)
+        ]
+
+    def stage_attended():
+        for h in range(GROUP):
+            part = slice(h * HEAD, (h + 1) * HEAD)
+            dot_t[h] = dobuf[:, part].T
+            o = (ot[h] * lrun[h]).astype(BF)
+            o_own[:, part] = o.T
+            delta[h] = jnp.sum(o.astype(F32) * dot_t[h].astype(F32), axis=0, keepdims=True)
+        for copy in att_copies():
+            copy.start()
+        own_att.start()
+
     def value_step(step, carry):
         reduce_step(step, value_term, vs, vr, rvsem, VALUE_HOPS)
+        pl.when(step == 1)(stage_attended)
         return carry
 
     lax.fori_loop(1, STEPS + 1, value_step, 0)
-    own_hid.wait()
-    arrive(to_hid, hsem)
     sibling = (y * 2 + 1 - c, ctx)
     hid_half = hid_r.at[:, :, lanes(c * BLK, BLK)]
     hid_copy2 = remote(hid_half, hid_half, csem, 0, sibling)
-    hid_copy2.start()
 
     def share(part, d):
         at = pl.ds(part * (BLK // len(VALUE_HOPS)), BLK // len(VALUE_HOPS))
@@ -378,11 +397,27 @@
 
     halves = (0, 1)
 
-    def y_copy(i, d):
+    def y_start(index):
+        return index * YROWS - jnp.maximum(index - 2, 0) * (YROWS - YLESS)
+
+    def by_size(index, act):
+        pl.when(index < 2)(lambda: act(YROWS))
+        pl.when(index >= 2)(lambda: act(YLESS))
+
+    def y_copy(i, d, size):
         to = (y + d) % 4
         return remote(
-            w_y.at[i, :, rows(to * YROWS, YROWS)], w_yr.at[i, d - 1], ysem, i * 3 + d - 1, (to * 2 + c, ctx)
+            w_y.at[i, :, rows(y_start(to), size)],
+            w_yr.at[i, d - 1, :, pl.ds(0, size)],
+            ysem,
+            i * 3 + d - 1,
+            (to * 2 + c, ctx),
         )
+
+    def stage_hidden():
+        own_hid.wait()
+        arrive(to_hid, hsem)
+        hid_copy2.start()
 
     def stage_product():
         hid_copy2.wait_recv()
@@ -395,45 +430,48 @@
                     def _():
                         wait_recv(dv_all.at[core, at, pl.ds(j * HEAD, HEAD)], gvsem, (part * 2 + j) * 2 + core)
 
-        w_y[:, :, ROWS:] = jnp.zeros((2, NZ, PAD - ROWS, HEAD), BF)
         h_rows = hid_r[...].reshape(NZ * ROWS, 2 * BLK)
         total = dot(h_rows, dv_all[...].reshape(2 * BLK, 256)).astype(BF)
         for i in halves:
-            w_y[i, :, :ROWS] = total[:, i * HEAD:(i + 1) * HEAD].reshape(NZ, ROWS, HEAD)
+            w_y[i] = total[:, i * HEAD:(i + 1) * HEAD].reshape(NZ, ROWS, HEAD)
             for d in range(1, 4):
-                y_copy(i, d).start()
-
-    def z_copy(i, d):
-        return remote(w_z.at[i, (z + d) % NZ], w_zr.at[i, d - 1], zsem, i * (NZ - 1) + d - 1, at_z(d))
-
-    def stage_z():
+                by_size((y + d) % 4, lambda size: y_copy(i, d, size).start())
+
+    def z_copy(i, d, size):
+        at = pl.ds(0, size)
+        return remote(
+            w_z.at[i, (z + d) % NZ, at], w_zr.at[i, d - 1, at], zsem, i * (NZ - 1) + d - 1, at_z(d)
+        )
+
+    def stage_z(size):
         for i in halves:
-            total = w_y[i, :, rows(y * YROWS, YROWS), :].astype(F32)
+            total = w_y[i, :, rows(y_start(y), size), :].astype(F32)
             for d in range(1, 4):
-                wait_recv(w_yr.at[i, d - 1], ysem, i * 3 + d - 1)
-                total += w_yr[i, d - 1].astype(F32)
-            w_z[i] = total.astype(BF)
+                wait_recv(w_yr.at[i, d - 1, :, pl.ds(0, size)], ysem, i * 3 + d - 1)
+                total += w_yr[i, d - 1, :, :size].astype(F32)
+            w_z[i, :, :size] = total.astype(BF)
             for d in range(1, NZ):
-                z_copy(i, d).start()
-
-    def f_copy(i, d):
-        target = w_all.at[c * 2 + i, rows(y * YROWS, YROWS)]
-        return remote(w_f.at[i], target, fsem, i * (NDP - 1) + d - 1, at_dp(d))
-
-    def stage_f():
+                z_copy(i, d, size).start()
+
+    def f_copy(i, d, size):
+        target = w_all.at[c * 2 + i, rows(y_start(y), size)]
+        return remote(w_f.at[i, pl.ds(0, size)], target, fsem, i * (NDP - 1) + d - 1, at_dp(d))
+
+    def stage_f(size):
         for i in halves:
-            total = w_z[i, z].astype(F32)
+            total = w_z[i, z, :size].astype(F32)
             for d in range(1, NZ):
-                wait_recv(w_zr.at[i, d - 1], zsem, i * (NZ - 1) + d - 1)
-                total += w_zr[i, d - 1].astype(F32)
-            w_f[i] = (total * (1.0 / math.sqrt(32768.0))).astype(BF)
-            w_all[c * 2 + i, rows(y * YROWS, YROWS), :] = w_f[i]
+                wait_recv(w_zr.at[i, d - 1, pl.ds(0, size)], zsem, i * (NZ - 1) + d - 1)
+                total += w_zr[i, d - 1, :size].astype(F32)
+            w_f[i, :size] = (total * (1.0 / math.sqrt(32768.0))).astype(BF)
+            w_all[c * 2 + i, rows(y_start(y), size), :] = w_f[i, :size]
             for d in range(1, NDP):
-                f_copy(i, d).start()
+                f_copy(i, d, size).start()
 
     def key_step(step, carry):
         reduce_step(step, key_term, ks, kr, rksem, KEY_HOPS)
-        pl.when(step == 1)(stage_product)
+        pl.when(step == 1)(stage_hidden)
+        pl.when(step == 2)(stage_product)
         return carry
 
     lax.fori_loop(1, STEPS + 1, key_step, 0)
@@ -444,29 +482,30 @@
     sent += exchange(lambda dst: dq_own.at[rows(dst * TOK, TOK)], to_dq, dqsem)
     own_dq = pltpu.make_async_copy(dq_own.at[mine], to_dq(x), lsem.at[0])
     own_dq.start()
-    stage_z()
-    reduce_last(lambda block, part, parts: last, dk_own, kr, rksem, KEY_HOPS)
+    by_size(y, stage_z)
+    reduce_last(lambda block, part, parts: last[part * (BLK // parts):(part + 1) * (BLK // parts)], dk_own, kr, rksem, KEY_HOPS)
     to_dk = lambda src: dk_out.at[:, lanes(src * HEAD, HEAD)]
     sent += exchange(lambda dst: dk_own.at[rows(dst * TOK, TOK)], to_dk, gksem)
     dk_out[:, lanes(x * HEAD, HEAD)] = dk_own[mine, :]
-    stage_f()
+    by_size(y, stage_f)
 
     own_dq.wait()
     own_att.wait()
     arrive(to_att, asem)
-    for copy in sent:
+    for copy in sent + att_copies():
         copy.wait_send()
     for buf, sems, hops in ((kbuf, ksem_r, K_HOPS), (vbuf, vsem_r, V_HOPS)):
         for up in (True, False):
             for step in range(1, hops[0 if up else 1] + 1):
-                ring_send(buf, sems, hops, up, step, lambda copy: copy.wait_send())
+                for part in range(hops[2]):
+                    ring_send(buf, sems, hops, up, step, part, lambda copy: copy.wait_send())
     reduce_sent(vs, vr, rvsem, VALUE_HOPS)
     reduce_sent(ks, kr, rksem, KEY_HOPS)
     for i in halves:
         for d in range(1, 4):
-            y_copy(i, d).wait_send()
+            by_size((y + d) % 4, lambda size: y_copy(i, d, size).wait_send())
         for d in range(1, NZ):
-            z_copy(i, d).wait_send()
+            by_size(y, lambda size: z_copy(i, d, size).wait_send())
     hid_copy2.wait_send()
     for part in range(len(VALUE_HOPS)):
         for d in range(1, NX):
@@ -478,9 +517,13 @@
     for i in halves:
         for d in range(1, NDP):
             src = (dp + NDP - d) % NDP
-            target = w_all.at[src % 2 * 2 + i, rows(src // 2 * YROWS, YROWS)]
-            wait_recv(target, fsem, i * (NDP - 1) + d - 1)
-            f_copy(i, d).wait_send()
+
+            def done(size):
+                target = w_all.at[src % 2 * 2 + i, rows(y_start(src // 2), size)]
+                wait_recv(target, fsem, i * (NDP - 1) + d - 1)
+
+            by_size(src // 2, done)
+            by_size(y, lambda size: f_copy(i, d, size).wait_send())
 
 
 def finish(att, dq, dk, dv, w, att_out, dq_out, dk_out, dv_out, w_out):
@@ -489,7 +532,7 @@
     dk_out[...] = dk[...].astype(F32)
     dv_out[...] = dv[...].astype(F32)
     for i in range(4):
-        w_out[:, i * HEAD:(i + 1) * HEAD] = w[i, :ROWS].astype(F32)
+        w_out[:, i * HEAD:(i + 1) * HEAD] = w[i].astype(F32)
 
 
 def per_device(hidden_in, value_weight, queries, keys, out_grad):
@@ -503,7 +546,7 @@
             jax.ShapeDtypeStruct((TOK, 2560), BF),
             jax.ShapeDtypeStruct((TOK, 512), BF),
             jax.ShapeDtypeStruct((TOK, 512), BF),
-            jax.ShapeDtypeStruct((4, PAD, HEAD), BF),
+            jax.ShapeDtypeStruct((4, ROWS, HEAD), BF),
         ],
         in_specs=[anywhere] * 5,
         out_specs=[anywhere, anywhere, vmem, vmem, vmem],
@@ -537,7 +580,7 @@
             pltpu.VMEM((BLK, HEAD), BF),
             pltpu.VMEM((BLK, HEAD), BF),
             pltpu.VMEM((2, BLK, 256), BF),
-            pltpu.VMEM((2, NZ, PAD, HEAD), BF),
+            pltpu.VMEM((2, NZ, ROWS, HEAD), BF),
             pltpu.VMEM((2, 3, NZ, YROWS, HEAD), BF),
             pltpu.VMEM((2, NZ, YROWS, HEAD), BF),
             pltpu.VMEM((2, NZ - 1, YROWS, HEAD), BF),
@@ -554,9 +597,9 @@
             dma((2, 3)),
             dma((2, 3)),
             dma((2, NZ - 1)),
-            dma((2, NZ - 1)),
+            dma((2, 2 * (NZ - 1))),
             dma((2, 4 * (NZ - 1))),
-            dma((2, NZ - 1)),
+            dma((2, 2 * (NZ - 1))),
             dma((2, 1)),
             dma((2, 6)),
             dma((2, 2 * (NZ - 1))),

time: 95.5 us -> 91.2 us (0.955)
  Pallas kernels: 93.5 us -> 89.5 us
    pallas_call x1, Pallas kernels: 90.5 us -> 86.5 us  [per_device(): pl.pallas_call(kernel, out_shape=[jax.ShapeDtypeStruct((TOK, 2560), BF),...]
where the time goes in v3:
time: 91.2 us; the launch traced here: 90.1 us
  Pallas kernels  89.5 us (98%)
    pallas_call x1, Pallas kernels, per_device(): pl.pallas_call(kernel, out_shape=[jax.ShapeDtypeStruct((TOK, 2560), BF),...  86.5 us
    pallas_call x1, Pallas kernels, per_device(): pl.pallas_call(finish, out_shape=[jax.ShapeDtypeStruct((TOK, 2560), BF),...  3.04 us

profile of v3, /device:TPU:2, one launch (start us, length us, event | category | flops | bytes accessed | tf_op | source)
XLA Modules:
  0.0 90.1 jit_solution(11203988197782186866)
XLA Ops:
  0.6 86.5 %shard_map.92 = (bf16[128,2560]{1,0:T(8,128)(2,1)}, bf16[128,2560]{1,0:T(8,128)(2,1)}, bf16[128,512]{1,0:T(8,128)(2,1)}, bf16[128,512]{1,0:T(8,128)(2,1)}, bf16[4,160,128]{2,1,0:T(8,128)(2,1)}) custom-call(bf16[128,5120]{1,0:T(8,128)(2,1)} %bitcast.8, bf16[5120,512]{1,0:T(8,128)(2,1)} %vw_in.1, bf16[128,2560]{1,0:T(8,128)(2,1)} %bitcast.9, ...), custom_call_target="tpu_custom_call" | custom-call | tf_op jit(solution)/shard_map/pallas_call | solution.py:542
  87.1 3.0 %shard_map.93 = (bf16[128,2560]{1,0:T(8,128)(2,1)}, f32[128,2560]{1,0:T(8,128)}, f32[128,512]{1,0:T(8,128)}, f32[128,512]{1,0:T(8,128)}, f32[160,512]{1,0:T(8,128)}) custom-call(bf16[128,2560]{1,0:T(8,128)(2,1)} %get-tuple-element.15.att, bf16[128,2560]{1,0:T(8,128)(2,1)} %get-tuple-element.16.dq, bf16[128,512]{1,0:T(8,128)(2,1)} %get-tuple-element.17.dk, ...), custom_call_target="tpu_custom_call" | custom-call | tf_op jit(solution)/shard_map/pallas_call | solution.py:612
